TPU v7x, 256 devices: a whole 4x4x8 slice. The times are simulated.
256 devices in a mesh: tile: 64 (over z_lo, x, y, core), mem: 4 (over z_hi).
Axes of the slice: x: 4, y: 4, z: 8 (z_hi: 4, z_lo: 2; z = z_hi * 2 + z_lo), core: 2. Of those that a mesh axis runs over, the one named last changes fastest.
Arguments:
- right_side: float32 [64, 256, 2048], P(None, 'tile'), may hold values from -6 to 6
- static_var: float32 [64, 256, 2048], P(None, 'tile'), may hold values from 0.3 to 3
- members: bfloat16 [20, 64, 1024, 128], P('mem', None, 'tile'), may hold values from -6 to 6
- vertical_root: float32 [64, 64], replicated, may hold values from -0.75 to 0.75
- stencil: int32 [512, 4], P('tile'), may hold values from 0 to 7
- weights: bfloat16 [4, 1024, 256], replicated, may hold values from -0.1875 to 0.1875
Outputs:
- solution_field: float32 [64, 256, 2048], P(None, 'tile')
- residual: float32 [64, 256, 2048], P(None, 'tile')
Inputs may be any that keep to these rules, and one draw needn't show every extreme that they name: `stencil`: entries number fine blocks of the same index of tile, in the local order coarse row within the device times 4 plus segment.
All inputs are finite; a program needn't handle non-finite values.
Results may differ from a plain program's by a relative error of at most 0.0085.
Values may be sent and summed in bfloat16 or wider, within the bound.
A program may use at most 128 MiB of HBM per device.

v0:
```python
import math

import jax
import jax.numpy as jnp
from jax import lax
from jax.sharding import PartitionSpec as P

BLOCK = 256
STENCIL = 4
REACH = 4
ITERS = 2


def extended(shard, sides, width):
    for axis, dim in sides:
        size, length = (lax.axis_size(axis), shard.shape[dim])
        up = [(i, (i + 1) % size) for i in range(size)]
        down = [(j, i) for i, j in up]
        last = lax.slice_in_dim(shard, length - width, length, axis=dim)
        first = lax.slice_in_dim(shard, 0, width, axis=dim)
        before = lax.ppermute(last, axis, up)
        after = lax.ppermute(first, axis, down)
        shard = jnp.concatenate([before, shard, after], axis=dim)
    return shard


def kernel_taps(reach):
    values = [math.exp(-(offset * offset) / (reach * reach)) for offset in range(-reach, reach + 1)]
    summed = sum(values)
    return [factor / summed for factor in values]


def fine_to_blocks(field_in, rows_count):
    levels = field_in.shape[0]
    segments = field_in.shape[2] // (2 * BLOCK)
    shaped = field_in.reshape(levels, rows_count, 2, segments, 2 * BLOCK)
    return shaped.transpose(1, 3, 0, 2, 4).reshape(rows_count * segments, levels, 4 * BLOCK)


def blocks_to_fine(blocks, rows_count, segments):
    levels = blocks.shape[1]
    shaped = blocks.reshape(rows_count, segments, levels, 2, 2 * BLOCK)
    return shaped.transpose(2, 0, 3, 1, 4).reshape(levels, 2 * rows_count, segments * 2 * BLOCK)


def coarse_to_grid(blocks, rows_count, segments):
    levels = blocks.shape[1]
    shaped = blocks.reshape(rows_count, segments, levels, BLOCK)
    return shaped.transpose(2, 1, 3, 0).reshape(levels, segments * BLOCK, rows_count)


def grid_to_coarse(grid, rows_count, segments):
    levels = grid.shape[0]
    shaped = grid.reshape(levels, segments, BLOCK, rows_count)
    return shaped.transpose(3, 1, 0, 2).reshape(rows_count * segments, levels, BLOCK)


def along_columns(widened, kernel):
    reach = (len(kernel) - 1) // 2
    inner_width = widened.shape[2] - 2 * reach
    summed = jnp.zeros(widened.shape[:2] + (inner_width,) + widened.shape[3:], jnp.float32)
    for offset in range(len(kernel)):
        summed = summed + kernel[offset] * widened[:, :, offset : offset + inner_width]
    return summed


def along_rows(data, kernel):
    reach = (len(kernel) - 1) // 2
    padded = jnp.pad(data, ((0, 0), (0, 0), (0, 0), (reach, reach)))
    length = data.shape[3]
    summed = jnp.zeros(data.shape, jnp.float32)
    for offset in range(len(kernel)):
        summed = summed + kernel[offset] * padded[:, :, :, offset : offset + length]
    return summed


def horizontal(weighted, kernel):
    for repeat in range(2):
        widened = extended(weighted.astype(jnp.bfloat16), (("tile", 2),), REACH).astype(
            weighted.dtype
        )
        weighted = along_rows(along_columns(widened, kernel), kernel)
    return weighted


def on_device(right_side, static_var, members, vertical_root, stencil, weights):
    kernel = kernel_taps(REACH)
    fine_rows = right_side.shape[1]
    fine_cols = right_side.shape[2]
    levels = right_side.shape[0]
    rows_dev = fine_rows // 2
    segments = fine_cols // (2 * BLOCK)
    block_count = rows_dev * segments
    member_count = members.shape[0] * lax.axis_size("mem")
    targets = jnp.arange(block_count, dtype=jnp.int32)
    onehots = [
        (stencil[:, position][None, :] == targets[:, None]).astype(jnp.float32)
        for position in range(STENCIL)
    ]
    member_float = members.astype(jnp.float32)

    def squares(vector_in):
        return lax.psum(jnp.sum(vector_in * vector_in), "tile")

    solution_field = jnp.zeros_like(right_side)
    residual = right_side
    direction = right_side
    norm_now = squares(residual)
    for iteration in range(ITERS):
        blocks = fine_to_blocks(direction.astype(jnp.bfloat16), rows_dev)
        coarse = jnp.zeros((block_count, levels, BLOCK), jnp.float32)
        for operate_position in range(STENCIL):
            coarse = coarse + jnp.einsum(
                "blf,fc->blc",
                blocks[stencil[:, operate_position]],
                weights[operate_position],
                preferred_element_type=jnp.float32,
            )
        grid = coarse_to_grid(coarse.astype(jnp.bfloat16), rows_dev, segments)
        ensemble_in = lax.all_to_all(grid, "tile", split_axis=1, concat_axis=2, tiled=True)
        weighted = member_float * ensemble_in.astype(jnp.float32)[None]
        weighted = jnp.einsum(
            "lk,mlxy->mkxy", vertical_root, weighted, precision=lax.Precision.HIGHEST
        )
        weighted = horizontal(weighted, kernel)
        weighted = jnp.einsum(
            "kl,mlxy->mkxy", vertical_root, weighted, precision=lax.Precision.HIGHEST
        )
        local_terms = jnp.sum(member_float * weighted, axis=0)
        whole_sum = lax.psum(local_terms.astype(jnp.bfloat16), "mem").astype(jnp.float32)
        whole_half = (whole_sum / (member_count - 1)).astype(jnp.bfloat16)
        returned = lax.all_to_all(whole_half, "tile", split_axis=2, concat_axis=1, tiled=True)
        back = grid_to_coarse(returned, rows_dev, segments)
        fine_blocks = jnp.zeros((block_count, levels, 4 * BLOCK), jnp.float32)
        for operate_position in range(STENCIL):
            update = jnp.einsum(
                "blc,fc->blf", back, weights[operate_position], preferred_element_type=jnp.float32
            )
            fine_blocks = fine_blocks + jnp.einsum(
                "jb,blf->jlf", onehots[operate_position], update, precision=lax.Precision.HIGHEST
            )
        prolonged = blocks_to_fine(fine_blocks, rows_dev, segments)
        product_image = direction + static_var * direction + prolonged
        step_size = norm_now / lax.psum(jnp.sum(direction * product_image), "tile")
        solution_field = solution_field + step_size * direction
        residual = residual - step_size * product_image
        norm_next = squares(residual)
        direction = residual + norm_next / norm_now * direction
        norm_now = norm_next
    return (solution_field, residual)


def solution(mesh):
    in_specs = (
        P(None, "tile", None),
        P(None, "tile", None),
        P("mem", None, "tile", None),
        P(),
        P("tile", None),
        P(),
    )
    out_specs = (P(None, "tile", None), P(None, "tile", None))
    return jax.shard_map(
        on_device, mesh=mesh, in_specs=in_specs, out_specs=out_specs, check_vma=False
    )
```

profile of v0, /device:TPU:1, one launch (start us, length us, event | category | flops | bytes accessed | tf_op | source)
XLA Modules:
  0.0 813.3 jit_solution(4313067124853454543)
XLA Ops:
  8.1 2.0 convert_element_type.105
  18.8 1.8 fusion.172
  24.3 19.9 %all_to_all.48 = bf16[64,2,1024]{2,1,0:T(2,128)(2,1)S(1)} all-to-all(bf16[64,2,1024]{2,1,0:T(2,128)(2,1)S(1)} %reshape.171), channel_id=1, replica_groups=mesh['tile'=64,'mem'=4] {'tile'}, dimensions={0} | all-to-all | bytes 524288 | tf_op jit(solution)/shard_map/all_to_all | solution.py:120
  45.8 2.4 copy.69
  48.2 3.8 fusion.126
  53.2 3.6 collective-permute-done
  56.8 3.2 collective-permute-done.1
  60.3 3.2 fusion.112
  63.5 5.6 fusion.13
  69.2 3.7 collective-permute-start.3
  73.9 1.9 collective-permute-done.3
  76.0 3.2 fusion.104
  79.2 9.2 %fusion.1 = bf16[64,16,128]{2,0,1:T(8,128)(2,1)} fusion(f32[5,64,16,128]{3,1,2,0:T(8,128)S(1)} %fusion.104, bf16[5,64,16,128]{3,2,1,0:T(8,128)(2,1)S(1)} %copy-done.5, f32[64,64]{1,0:T(8,128)S(1)} %copy-done), kind=kOutput, calls=%fused_computation.47 | convolution fusion | flops 516292608 | bytes 4210688 | tf_op jit(solution)/shard_map/kl,mlxy->mkxy/dot_general | solution.py:126
  88.6 58.5 %all-reduce.8.cloned.1.call-done = bf16[64,16,128]{2,0,1:T(8,128)(2,1)} async-done(((bf16[64,16,128]{2,0,1:T(8,128)(2,1)}), bf16[64,16,128]{2,0,1:T(8,128)(2,1)}) %all-reduce.8.cloned.1.call-update) | async-done | bytes 262160 | tf_op jit(solution)/shard_map/psum | solution.py:130
  148.9 19.6 %all_to_all.49 = bf16[64,2,1024]{2,1,0:T(2,128)(2,1)S(1)} all-to-all(bf16[64,2,1024]{2,1,0:T(2,128)(2,1)S(1)} %reshape.173), channel_id=1, replica_groups=mesh['tile'=64,'mem'=4] {'tile'}, dimensions={0} | all-to-all | bytes 524288 | tf_op jit(solution)/shard_map/all_to_all | solution.py:132
  174.3 2.8 add_add_fusion.1
  177.1 3.0 reshape.82
  180.1 1.9 copy.78
  182.0 4.1 reshape.83
  186.2 4.1 multiply_reduce_fusion.2
  190.2 139.1 %all-reduce.4 = (f32[]{:T(128)}, f32[]{:T(128)}) all-reduce(f32[]{:T(128)} %get-tuple-element.3, f32[]{:T(128)} %get-tuple-element.2), channel_id=1, replica_groups=mesh['tile'=64,'mem'=4] {'tile'}, use_global_device_ids=true, to_apply=%region_1.0 | all-reduce | flops 2 | bytes 16 | tf_op jit(solution)/shard_map/psum | solution.py:103
  330.6 5.6 multiply_reduce_fusion.1
  336.2 140.1 %psum.45 = f32[]{:T(128)} all-reduce(f32[]{:T(128)} %get-tuple-element.6), channel_id=1, replica_groups=mesh['tile'=64,'mem'=4] {'tile'}, use_global_device_ids=true, to_apply=%region_7.8 | all-reduce | flops 1 | bytes 8 | tf_op jit(solution)/shard_map/psum | solution.py:103
  477.6 3.4 fusion.236
  482.8 1.8 copy.123
  484.5 1.8 reshape.85
  492.7 1.9 fusion.168
  494.7 1.9 convolution_add_fusion.2
  498.5 13.7 %all_to_all.50 = bf16[64,2,1024]{2,1,0:T(2,128)(2,1)S(1)} all-to-all(bf16[64,2,1024]{2,1,0:T(2,128)(2,1)S(1)} %reshape.175), channel_id=1, replica_groups=mesh['tile'=64,'mem'=4] {'tile'}, dimensions={0} | all-to-all | bytes 524288 | tf_op jit(solution)/shard_map/all_to_all | solution.py:120
  513.9 2.4 copy.84
  516.3 3.8 fusion.127
  521.2 3.6 collective-permute-done.4
  524.9 3.2 collective-permute-done.5
  528.3 3.2 fusion.96
  531.5 5.6 fusion.55
  537.2 3.9 collective-permute-start.7
  541.9 2.0 collective-permute-done.7
  544.3 3.2 fusion.88
  547.4 9.2 %fusion.3 = bf16[64,16,128]{2,0,1:T(8,128)(2,1)} fusion(f32[5,64,16,128]{3,1,2,0:T(8,128)S(1)} %fusion.88, bf16[5,64,16,128]{3,2,1,0:T(8,128)(2,1)S(1)} %copy-done.6, f32[64,64]{1,0:T(8,128)S(1)} %copy-done), kind=kOutput, calls=%fused_computation.49 | convolution fusion | flops 516292608 | bytes 4210688 | tf_op jit(solution)/shard_map/kl,mlxy->mkxy/dot_general | solution.py:126
  556.6 55.5 %all-reduce.10.cloned.1.call-done = bf16[64,16,128]{2,0,1:T(8,128)(2,1)} async-done(((bf16[64,16,128]{2,0,1:T(8,128)(2,1)}), bf16[64,16,128]{2,0,1:T(8,128)(2,1)}) %all-reduce.10.cloned.1.call-update) | async-done | bytes 262160 | tf_op jit(solution)/shard_map/psum | solution.py:130
  613.9 19.8 %all_to_all.51 = bf16[64,2,1024]{2,1,0:T(2,128)(2,1)S(1)} all-to-all(bf16[64,2,1024]{2,1,0:T(2,128)(2,1)S(1)} %reshape.177), channel_id=1, replica_groups=mesh['tile'=64,'mem'=4] {'tile'}, dimensions={0} | all-to-all | bytes 524288 | tf_op jit(solution)/shard_map/all_to_all | solution.py:132
  640.8 2.6 add_add_fusion
  643.4 4.0 reshape.90
  647.5 3.7 copy.93
  651.1 4.0 reshape.91
  655.2 5.0 multiply_reduce_fusion
  660.1 138.8 %psum.47 = f32[]{:T(128)} all-reduce(f32[]{:T(128)} %multiply_reduce_fusion), channel_id=1, replica_groups=mesh['tile'=64,'mem'=4] {'tile'}, use_global_device_ids=true, to_apply=%region_11.12 | all-reduce | flops 1 | bytes 8 | tf_op jit(solution)/shard_map/psum | solution.py:144
  800.2 6.0 multiply_subtract_fusion
  (102 shorter events, 48.5 us)
Async XLA Ops:
  7.2 41.1 %copy-start = (f32[64,64]{1,0:T(8,128)S(1)}, f32[64,64]{1,0:T(8,128)}, u32[]{:S(2)}) copy-start(f32[64,64]{1,0:T(8,128)} %param.9) | copy-start | bytes 49156
  7.2 139.9 %all-reduce.8.cloned.1.call-start = ((), (), s32[]{:S(2)}) async-start(), calls=%async_computation.4 | async-start | bytes 524288 | tf_op jit(solution)/shard_map/psum | solution.py:130
  15.6 3.2 copy-start.2
  18.8 3.5 copy-start.10
  20.6 2.2 copy-start.8
  44.6 3.6 copy-start.5
  52.1 4.7 collective-permute-start
  52.7 7.2 collective-permute-start.1
  69.1 4.8 collective-permute-start.2
  69.2 6.6 collective-permute-start.3
  88.4 523.7 %all-reduce.10.cloned.1.call-start = ((), (), s32[]{:S(2)}) async-start(), calls=%async_computation.5 | async-start | bytes 524288 | tf_op jit(solution)/shard_map/psum | solution.py:130
  182.0 4.1 copy-start.1
  492.7 3.9 copy-start.3
  492.7 3.9 copy-start.9
  494.7 2.4 copy-start.7
  512.7 3.6 copy-start.6
  520.2 4.7 collective-permute-start.4
  520.8 7.2 collective-permute-start.5
  537.1 4.8 collective-permute-start.6
  537.2 6.7 collective-permute-start.7
  634.4 1.8 copy-start.4
Sparse Core Ops, SparseCore 0:
  88.5 58.5 all-reduce.7
  556.8 55.3 all-reduce.9
where the time goes:
time: 822 us; the launch traced here: 813 us
  blocking collectives  491 us (60%)
  waiting for transfers between devices  133 us (16%)
  other arithmetic  54.1 us (7%)
  local copies, waits for them, and re-layouts  54 us (7%)
  matrix products  51.9 us (6%)
  between operations  18.7 us (2%)
  starting transfers between devices  10.1 us (1%)
    psum x2, blocking collectives, squares(): return lax.psum(jnp.sum(vector_in * vector_in), 'tile')  279 us
    psum x1, blocking collectives, on_device(): step_size = norm_now / lax.psum(jnp.sum(direction * product_image), 'tile')  139 us
    psum x2, waiting for transfers between devices, on_device(): lax.psum(local_terms.astype(jnp.bfloat16), 'mem').astype(jnp.float32)  114 us
    all_to_all x2, blocking collectives, on_device(): lax.all_to_all(whole_half, 'tile', split_axis=2, concat_axis=1, tiled=True)  39.5 us
    all_to_all x2, blocking collectives, on_device(): lax.all_to_all(grid, 'tile', split_axis=1, concat_axis=2, tiled=True)  33.6 us
    dot_general x2, matrix products, on_device(): jnp.einsum('kl,mlxy->mkxy', vertical_root, weighted, precision=lax.Precis...  18.4 us
  transfers between devices with their start and end apart: 10, of which 10 were waited for; matrix products, arithmetic and copies ran while one was open for 0% of the time, Pallas kernels for 0%

commit v1 on v0

v1 whole, which is shorter than its diff:
```python
import functools
import math

import jax
import jax.numpy as jnp
import numpy as np
from jax import lax
from jax.experimental import pallas as pl
from jax.experimental.pallas import tpu as pltpu
from jax.sharding import PartitionSpec as P

LEV = 64
COLS = 1024
BLOCK = 256
STENCIL = 4
REACH = 4
MEMBERS = 20
ROWS = 128
TILES = 64
MEMS = 4
LOCAL = 5
WIDTH = 16
QUARTER = TILES // MEMS
PAIRS = 32
MESH = pl.DeviceIdType.MESH
F32 = jnp.float32
BF16 = jnp.bfloat16


def kernel_taps(reach):
    values = [math.exp(-(offset * offset) / (reach * reach)) for offset in range(-reach, reach + 1)]
    summed = sum(values)
    return np.array([factor / summed for factor in values])


def row_operator():
    taps = kernel_taps(REACH)
    once = np.zeros((ROWS, ROWS))
    for row in range(ROWS):
        for offset in range(-REACH, REACH + 1):
            if 0 <= row + offset < ROWS:
                once[row, row + offset] = taps[offset + REACH]
    return once @ once


def row_blocks():
    twice = row_operator()
    kinds = []
    for group, shifts in ((8, range(-2, 3)), (0, range(0, 3)), (31, range(-2, 1))):
        for shift in shifts:
            at = 4 * (group + shift)
            kinds.append(twice[4 * group : 4 * group + 4, at : at + 4].T)
    return np.stack(kinds)


def column_operator():
    taps = kernel_taps(REACH)
    twice = np.convolve(taps, taps)
    places = list(range(WIDTH)) + list(range(-8, 0)) + list(range(WIDTH, WIDTH + 8))
    out = np.zeros((WIDTH, 2 * WIDTH))
    for to in range(WIDTH):
        for at, place in enumerate(places):
            if abs(place - to) <= 2 * REACH:
                out[to, at] = twice[place - to + 2 * REACH]
    return np.kron(np.eye(8), out)


def kernel(
    b_hbm, s_hbm, mem_hbm, amat_hbm, xop_hbm, st_ref, w_hbm, sol_hbm, res_hbm,
    bv, sv, ab, mem, amat, xop, wv, fb, onehot, send_c, recv_c, own_c, u, ens, es, rs, zs, back, hs, outv,
    part, sc1, sc2, sc3,
    load_sem, a_send, a_recv, b_send, b_recv, c_send, c_recv, s_send, s_recv, out_sem,
):
    me = lax.axis_index("tile")
    mm = lax.axis_index("mem")

    def at_tile(t):
        return {"tile": t, "mem": mm}

    def at_mem(m):
        return {"tile": me, "mem": m}

    barrier = pltpu.get_barrier_semaphore()

    def greet(k, carry):
        pl.semaphore_signal(barrier, inc=1, device_id=at_tile(lax.rem(me + k, TILES)), device_id_type=MESH)
        return carry

    lax.fori_loop(1, TILES, greet, 0)
    for k in range(1, MEMS):
        pl.semaphore_signal(barrier, inc=1, device_id=at_mem(lax.rem(mm + k, MEMS)), device_id_type=MESH)

    loads = []
    for r in range(4):
        loads.append(pltpu.make_async_copy(b_hbm.at[:, r, :], bv.at[r], load_sem.at[r]))
    loads.append(pltpu.make_async_copy(w_hbm, wv, load_sem.at[4]))
    for r in range(4):
        loads.append(pltpu.make_async_copy(s_hbm.at[:, r, :], sv.at[r], load_sem.at[5 + r]))
    loads.append(pltpu.make_async_copy(mem_hbm, mem, load_sem.at[9]))
    loads.append(pltpu.make_async_copy(amat_hbm, amat, load_sem.at[10]))
    loads.append(pltpu.make_async_copy(xop_hbm, xop, load_sem.at[11]))
    for load in loads:
        load.start()

    rows_at = lax.broadcasted_iota(jnp.int32, (LEV, 2 * LEV), 0)
    lanes_at = lax.broadcasted_iota(jnp.int32, (LEV, 2 * LEV), 1)
    eye0 = (lanes_at == rows_at).astype(F32)
    eye1 = (lanes_at == rows_at + LEV).astype(F32)
    for s in range(STENCIL):
        for q in range(4):
            e0 = st_ref[q, s]
            e1 = st_ref[4 + q, s]

            def place(j, carry, s=s, q=q, e0=e0, e1=e1):
                h0 = jnp.where(e0 == j, 1.0, 0.0).astype(F32)
                h1 = jnp.where(e1 == j, 1.0, 0.0).astype(F32)
                onehot[pl.ds(pl.multiple_of((s * 8 + j) * LEV, LEV), LEV), q * 128 : q * 128 + 128] = (
                    eye0 * h0 + eye1 * h1
                ).astype(BF16)
                return carry

            lax.fori_loop(0, 8, place, 0)
    for m in range(LOCAL):
        u[m, 0:32, :] = jnp.zeros((32, 256), BF16)
        u[m, 544:576, :] = jnp.zeros((32, 256), BF16)

    def pack_row(v):
        return jnp.sum(v.reshape(-1, 8, 128), axis=0).sum(axis=0, keepdims=True)

    def restrict(it):
        acc = None
        for s in range(STENCIL):
            rows = []
            for q in range(4):
                for i in range(2):
                    rows.append(fb[st_ref[4 * i + q, s]])
            term = jnp.dot(jnp.concatenate(rows, axis=0), wv[s], preferred_element_type=F32)
            acc = term if acc is None else acc + term
        for q in range(4):
            turned = acc[q * 128 : q * 128 + 128].T
            own_c[q * 256 : q * 256 + 256, :] = turned
        grid = own_c[...].reshape(TILES, 2, 8, 128)
        first, last = grid[:, 0], grid[:, 1]
        before = jnp.concatenate([last[TILES - 1 :], last[: TILES - 1]], axis=0)
        after = jnp.concatenate([first[1:], first[:1]], axis=0)
        send_c[it, :, 0:16, :] = jnp.concatenate([first, last], axis=1).astype(BF16)
        send_c[it, :, 16:32, :] = jnp.concatenate([before, after], axis=1).astype(BF16)

    def fill_blocks(r, field):
        p, rr = r // 2, r % 2
        for q in range(4):
            fb[4 * p + q, :, rr * 512 : rr * 512 + 512] = field[:, q * 512 : q * 512 + 512]

    mine = lax.rem(me, 2) * PAIRS + lax.div(me, 2)

    def wait_bytes(ref, sem):
        pltpu.make_async_copy(ref, ref, sem).wait()

    def c_copy(it, t):
        return pltpu.make_async_remote_copy(
            src_ref=send_c.at[it, t],
            dst_ref=recv_c.at[it, mine],
            send_sem=a_send.at[it],
            recv_sem=a_recv.at[it],
            device_id=at_tile(t),
            device_id_type=MESH,
        )

    def start_c(it):
        def go(k, carry):
            c_copy(it, lax.rem(me + k, TILES)).start()
            return carry

        lax.fori_loop(1, TILES, go, 0)
        recv_c[it, mine] = send_c[it, me]

    def wait_c(it):
        wait_bytes(recv_c.at[it, 0 : TILES - 1], a_recv.at[it])
        wait_bytes(send_c.at[it, 0 : TILES - 1], a_send.at[it])

    low = lax.rem(me, 8)
    high = lax.div(me, 8)

    def sum_copy(x, stage, k):
        if stage == 0:
            slot, dst = low, sc1
            to = at_tile(high * 8 + lax.rem(low + k, 8))
        elif stage == 1:
            slot, dst = high, sc2
            to = at_tile(lax.rem(high + k, 8) * 8 + low)
        else:
            slot, dst = mm, sc3
            to = at_mem(lax.rem(mm + k, MEMS))
        return pltpu.make_async_remote_copy(
            src_ref=part.at[x, stage],
            dst_ref=dst.at[x, slot],
            send_sem=s_send.at[x, stage],
            recv_sem=s_recv.at[x, stage],
            device_id=to,
            device_id_type=MESH,
        )

    def sum_start(x, stage, value):
        part[x, stage] = value
        if stage == 0:
            sc1[x, low] = value
        elif stage == 1:
            sc2[x, high] = value
        else:
            sc3[x, mm] = value

        def go(k, carry):
            sum_copy(x, stage, k).start()
            return carry

        lax.fori_loop(1, MEMS if stage == 2 else 8, go, 0)

    def sum_end(x, stage):
        held = (sc1, sc2, sc3)[stage]
        count = MEMS - 1 if stage == 2 else 7
        wait_bytes(held.at[x, 0:count], s_recv.at[x, stage])
        wait_bytes(held.at[x, 0:count], s_send.at[x, stage])
        return jnp.sum(held[x], axis=0)

    def stack_rows(rows):
        rows = rows + [jnp.zeros((8 - len(rows), 128), F32)]
        return jnp.concatenate(rows, axis=0)

    def pick(tile, row):
        return jnp.sum(tile[row : row + 1, :], axis=1, keepdims=True)

    def ensemble(it):
        def member(m, carry):
            for g in range(4):
                lanes = []
                for par in range(2):
                    w = mem[m, par, 8 * g : 8 * g + 8] * recv_c[it, par * PAIRS + 8 * g : par * PAIRS + 8 * g + 8]
                    lanes.append(w.reshape(256, 128))
                mixed = jnp.dot(xop[...], jnp.concatenate(lanes, axis=1), preferred_element_type=F32)
                u[m, 32 + 128 * g : 160 + 128 * g, :] = mixed.astype(BF16)
            for g in range(4):
                at = 32 + 128 * g
                wide = jnp.concatenate([u[m, at + 16 * d : at + 16 * d + 128, :] for d in range(-2, 3)], axis=1)
                inner = jnp.dot(wide, amat[0:1280, :], preferred_element_type=F32)
                if g == 0:
                    edge = jnp.concatenate([u[m, 32 + 16 * d : 48 + 16 * d, :] for d in range(0, 3)], axis=1)
                    edge = jnp.dot(edge, amat[1280:2048, :], preferred_element_type=F32)
                    inner = jnp.concatenate([edge, inner[16:]], axis=0)
                if g == 3:
                    edge = jnp.concatenate([u[m, 528 + 16 * d : 544 + 16 * d, :] for d in range(-2, 1)], axis=1)
                    edge = jnp.dot(edge, amat[2048:2816, :], preferred_element_type=F32)
                    inner = jnp.concatenate([inner[:112], edge], axis=0)
                for par in range(2):
                    own = mem[m, par, 8 * g : 8 * g + 8, 0:16, :].astype(F32)
                    term = own * inner[:, par * 128 : par * 128 + 128].reshape(8, 16, 128)
                    ens[par, 8 * g : 8 * g + 8] += term
            return carry

        ens[...] = jnp.zeros_like(ens)
        lax.fori_loop(0, LOCAL, member, 0)
        es[it] = jnp.stack([ens[0], ens[1]], axis=1).reshape(TILES, 16, 128).astype(BF16)

    def rs_copy(it, k):
        to = lax.rem(mm + k, MEMS)
        return pltpu.make_async_remote_copy(
            src_ref=es.at[it, pl.ds(to * QUARTER, QUARTER)],
            dst_ref=rs.at[it, mm],
            send_sem=b_send.at[it],
            recv_sem=b_recv.at[it],
            device_id=at_mem(to),
            device_id_type=MESH,
        )

    def start_rs(it):
        for k in (2, 1, 3):
            rs_copy(it, k).start()
        rs[it, mm] = es[it, pl.ds(mm * QUARTER, QUARTER)]

    def wait_rs(it):
        wait_bytes(rs.at[it, 0 : MEMS - 1], b_recv.at[it])
        wait_bytes(rs.at[it, 0 : MEMS - 1], b_send.at[it])
        total = rs[it, 0].astype(F32)
        for m in range(1, MEMS):
            total = total + rs[it, m].astype(F32)
        zs[it] = total.astype(BF16)

    def back_copy(it, tt, m):
        return pltpu.make_async_remote_copy(
            src_ref=zs.at[it, tt],
            dst_ref=back.at[it, me],
            send_sem=c_send.at[it],
            recv_sem=c_recv.at[it],
            device_id={"tile": mm * QUARTER + tt, "mem": m},
            device_id_type=MESH,
        )

    def start_back(it):
        def go(k, carry):
            m = lax.rem(mm + lax.div(k, QUARTER), MEMS)
            tt = lax.rem(me + k, QUARTER)
            itself = jnp.logical_and(mm * QUARTER + tt == me, m == mm)

            @pl.when(jnp.logical_not(itself))
            def _():
                back_copy(it, tt, m).start()

            @pl.when(itself)
            def _():
                pltpu.make_async_copy(zs.at[it, tt], back.at[it, me], c_recv.at[it]).start()

            return carry

        lax.fori_loop(0, TILES, go, 0)

    def wait_back(it):
        wait_bytes(back.at[it], c_recv.at[it])
        to_self = lax.div(me, QUARTER) == mm

        @pl.when(to_self)
        def _():
            wait_bytes(back.at[it, 0 : TILES - 1], c_send.at[it])

        @pl.when(jnp.logical_not(to_self))
        def _():
            wait_bytes(back.at[it], c_send.at[it])

    def gather_back(it):
        wide = jnp.concatenate([back[it, 16 * q : 16 * q + 16].reshape(256, 128) for q in range(4)], axis=1)
        for s in range(STENCIL):
            hs[s] = lax.dot_general(
                onehot[s * 512 : s * 512 + 512, :], wide, (((1,), (1,)), ((), ())), preferred_element_type=F32
            ).astype(BF16)

    def prolong(piece):
        total = None
        for s in range(STENCIL):
            term = lax.dot_general(
                hs[s],
                wv[s, piece * 256 : piece * 256 + 256, :],
                (((1,), (1,)), ((), ())),
                preferred_element_type=F32,
            )
            total = term if total is None else total + term
        return total

    for r in range(4):
        loads[r].wait()
        fill_blocks(r, bv[r].astype(BF16))
    loads[4].wait()
    restrict(0)
    pl.semaphore_wait(barrier, TILES - 1 + MEMS - 1)
    start_c(0)
    for r in range(4):
        loads[5 + r].wait()
    square = jnp.zeros((1, 128), F32)
    diag = jnp.zeros((1, 128), F32)
    for r in range(4):
        v = bv[r]
        square = square + pack_row(v * v)
        diag = diag + pack_row(v * v * (1.0 + sv[r]))
    sum_start(0, 0, stack_rows([square, diag]))
    for load in loads[9:]:
        load.wait()
    sum_start(0, 1, sum_end(0, 0))
    first_sums = sum_end(0, 1)
    wait_c(0)
    ensemble(0)
    start_rs(0)

    def col_dot(c_it):
        v = jnp.zeros((1, 128), F32)
        for par in range(2):
            v = v + pack_row(ens[par] * recv_c[c_it, par * PAIRS : par * PAIRS + PAIRS, 0:16, :].astype(F32))
        return v

    sum_start(1, 0, stack_rows([col_dot(0)]))
    wait_rs(0)
    start_back(0)
    sum_start(1, 1, sum_end(1, 0))
    sum_start(1, 2, sum_end(1, 1))
    second_sums = sum_end(1, 2)
    rr = pick(first_sums, 0)
    dad = pick(first_sums, 1) + pick(second_sums, 0)
    alpha = rr / dad
    wait_back(0)
    gather_back(0)
    square = jnp.zeros((1, 128), F32)
    diag = jnp.zeros((1, 128), F32)
    cross = jnp.zeros((1, 128), F32)
    for piece in range(4):
        rr_, half = piece // 2, piece % 2
        total = prolong(piece)
        for p in range(2):
            for q in range(4):
                r = 2 * p + rr_
                cols = slice(q * 512 + half * 256, q * 512 + half * 256 + 256)
                j = 4 * p + q
                d = bv[r, :, cols]
                factor = 1.0 + sv[r, :, cols]
                image = d * factor + total[j * 64 : j * 64 + 64, :]
                ab[r, :, cols] = image
                rnew = d - alpha * image
                fb[j, :, piece * 256 : piece * 256 + 256] = rnew.astype(BF16)
                square = square + pack_row(rnew * rnew)
                diag = diag + pack_row(rnew * rnew * factor)
                cross = cross + pack_row(d * rnew * factor)
    restrict(1)
    start_c(1)
    sum_start(2, 0, stack_rows([square, diag, cross]))
    sum_start(2, 1, sum_end(2, 0))
    third_sums = sum_end(2, 1)
    wait_c(1)
    ensemble(1)
    start_rs(1)
    sum_start(3, 0, stack_rows([col_dot(1), col_dot(0)]))
    wait_rs(1)
    start_back(1)
    sum_start(3, 1, sum_end(3, 0))
    sum_start(3, 2, sum_end(3, 1))
    fourth_sums = sum_end(3, 2)
    new = pick(third_sums, 0)
    beta = new / rr
    both = pick(third_sums, 2) + pick(fourth_sums, 1)
    dad2 = pick(third_sums, 1) + pick(fourth_sums, 0) + 2.0 * beta * both + beta * beta * dad
    alpha2 = new / dad2
    wait_back(1)
    gather_back(1)
    for piece in range(4):
        rr_, half = piece // 2, piece % 2
        total = prolong(piece)
        for p in range(2):
            for q in range(4):
                r = 2 * p + rr_
                cols = slice(q * 512 + half * 256, q * 512 + half * 256 + 256)
                j = 4 * p + q
                d = bv[r, :, cols]
                image = ab[r, :, cols]
                rnew = d - alpha * image
                second = rnew * (1.0 + sv[r, :, cols]) + total[j * 64 : j * 64 + 64, :] + beta * image
                outv[0, r, :, cols] = alpha * d + alpha2 * (rnew + beta * d)
                outv[1, r, :, cols] = rnew - alpha2 * second
    stores = []
    for r in range(4):
        stores.append(pltpu.make_async_copy(outv.at[0, r], sol_hbm.at[:, r, :], out_sem.at[r]))
        stores.append(pltpu.make_async_copy(outv.at[1, r], res_hbm.at[:, r, :], out_sem.at[4 + r]))
    for store in stores:
        store.start()
    for store in stores:
        store.wait()


def on_device(right_side, static_var, members, vertical_root, stencil, weights):
    turned = members.reshape(LOCAL, LEV, WIDTH, PAIRS, 2, 2).transpose(0, 4, 3, 2, 5, 1)
    turned = turned.reshape(LOCAL, 2, PAIRS, WIDTH, 128)
    up = [(i, (i + 1) % TILES) for i in range(TILES)]
    down = [(j, i) for i, j in up]
    before = lax.ppermute(turned[:, :, :, 8:], "tile", up)
    after = lax.ppermute(turned[:, :, :, :8], "tile", down)
    extended = jnp.concatenate([turned, before, after], axis=3)
    both = jnp.einsum("kl,jl->kj", vertical_root, vertical_root, precision=lax.Precision.HIGHEST)
    both = both / (MEMBERS - 1)
    blocks = jnp.asarray(row_blocks(), F32)
    amat = (blocks[:, :, None, :, None] * both[None, None, :, None, :]).reshape(11 * 256, 256).astype(BF16)
    xop = jnp.asarray(column_operator(), BF16)
    anyspec = pl.BlockSpec(memory_space=pl.ANY)
    field = jax.ShapeDtypeStruct(right_side.shape, F32)
    return pl.pallas_call(
        kernel,
        out_shape=(field, field),
        in_specs=[anyspec] * 5 + [pl.BlockSpec(memory_space=pltpu.SMEM), anyspec],
        out_specs=(anyspec, anyspec),
        scratch_shapes=[
            pltpu.VMEM((4, LEV, 2048), F32),
            pltpu.VMEM((4, LEV, 2048), F32),
            pltpu.VMEM((4, LEV, 2048), F32),
            pltpu.VMEM((LOCAL, 2, PAIRS, 32, 128), BF16),
            pltpu.VMEM((11 * 256, 256), BF16),
            pltpu.VMEM((128, 256), BF16),
            pltpu.VMEM((STENCIL, 1024, 256), BF16),
            pltpu.VMEM((8, LEV, 1024), BF16),
            pltpu.VMEM((2048, 512), BF16),
            pltpu.VMEM((2, TILES, 32, 128), BF16),
            pltpu.VMEM((2, TILES, 32, 128), BF16),
            pltpu.VMEM((COLS, 128), F32),
            pltpu.VMEM((LOCAL, 576, 256), BF16),
            pltpu.VMEM((2, PAIRS, 16, 128), F32),
            pltpu.VMEM((2, TILES, 16, 128), BF16),
            pltpu.VMEM((2, MEMS, QUARTER, 16, 128), BF16),
            pltpu.VMEM((2, QUARTER, 16, 128), BF16),
            pltpu.VMEM((2, TILES, 16, 128), BF16),
            pltpu.VMEM((STENCIL, 512, 256), BF16),
            pltpu.VMEM((2, 4, LEV, 2048), F32),
            pltpu.VMEM((4, 3, 8, 128), F32),
            pltpu.VMEM((4, 8, 8, 128), F32),
            pltpu.VMEM((4, 8, 8, 128), F32),
            pltpu.VMEM((4, MEMS, 8, 128), F32),
            pltpu.SemaphoreType.DMA((12,)),
            pltpu.SemaphoreType.DMA((2,)),
            pltpu.SemaphoreType.DMA((2,)),
            pltpu.SemaphoreType.DMA((2,)),
            pltpu.SemaphoreType.DMA((2,)),
            pltpu.SemaphoreType.DMA((2,)),
            pltpu.SemaphoreType.DMA((2,)),
            pltpu.SemaphoreType.DMA((4, 3)),
            pltpu.SemaphoreType.DMA((4, 3)),
            pltpu.SemaphoreType.DMA((8,)),
        ],
        compiler_params=pltpu.CompilerParams(
            collective_id=0, has_side_effects=True, vmem_limit_bytes=56 * 1024 * 1024
        ),
        name="conjugate_gradient",
    )(right_side, static_var, extended, amat, xop, stencil, weights)


def solution(mesh):
    in_specs = (
        P(None, "tile", None),
        P(None, "tile", None),
        P("mem", None, "tile", None),
        P(),
        P("tile", None),
        P(),
    )
    out_specs = (P(None, "tile", None), P(None, "tile", None))
    return jax.shard_map(on_device, mesh=mesh, in_specs=in_specs, out_specs=out_specs, check_vma=False)
```

time: 822 us -> 132 us (0.16)
  blocking collectives: 491 us -> 0 us
  waiting for transfers between devices: 133 us -> 0.62 us
  Pallas kernels: 0 us -> 92.5 us
  matrix products: 51.9 us -> 0.18 us
  other arithmetic: 54.1 us -> 4.98 us
  local copies, waits for them, and re-layouts: 54 us -> 27.3 us
  between operations: 18.7 us -> 0.69 us
    psum x3 -> x0, blocking collectives: 418 us -> none  [the longest x2 279 us: squares(): return lax.psum(jnp.sum(vector_in * vector_in), 'tile')]
    psum x2 -> x0, waiting for transfers between devices: 114 us -> none  [on_device(): lax.psum(local_terms.astype(jnp.bfloat16), 'mem').astype(jnp.float32)]
    pallas_call x0 -> x1, Pallas kernels: none -> 92.5 us  [on_device(): pl.pallas_call(kernel, out_shape=(field, field), in_specs=[anyspec] * 5 +...]
    all_to_all x4 -> x0, blocking collectives: 73.1 us -> none  [the longest x2 39.5 us: on_device(): lax.all_to_all(whole_half, 'tile', split_axis=2, concat_axis=1, tiled=True)]
    dot_general x28 -> x1, matrix products: 51.9 us -> 0.18 us  [on_device(): jnp.einsum('kl,jl->kj', vertical_root, vertical_root, precision=lax.Preci...]
    reshape x16 -> x1, local copies, waits for them, and re-layouts: 24.7 us -> 4.56 us  [on_device(): turned = turned.reshape(LOCAL, 2, PAIRS, WIDTH, 128)]
    ppermute x8 -> x2, waiting for transfers between devices: 19.4 us -> 0.62 us  [the longest x1 0.61 us: on_device(): after = lax.ppermute(turned[:, :, :, :8], 'tile', down)]
    convert_element_type x12 -> x1, other arithmetic: 20 us -> 3 us  [on_device(): (blocks[:, :, None, :, None] * both[None, None, :, None, :]).reshape(11 *...]
  transfers between devices with their start and end apart: 10 -> 2, of which waited for: 10 -> 1; matrix products, arithmetic and copies ran while one was open for 0% -> 7% of each run, Pallas kernels for 0% -> 0%
where the time goes in v1:
time: 132 us; the launch traced here: 130 us
  Pallas kernels  92.5 us (70%)
  local copies, waits for them, and re-layouts  27.3 us (21%)
  other arithmetic  4.98 us (4%)
  starting transfers between devices  3.24 us (2%)
    pallas_call x1, Pallas kernels, on_device(): pl.pallas_call(kernel, out_shape=(field, field), in_specs=[anyspec] * 5 +...  92.5 us
    unnamed x12, local copies, waits for them, and re-layouts  10.4 us
    transpose x1, local copies, waits for them, and re-layouts, on_device(): members.reshape(LOCAL, LEV, WIDTH, PAIRS, 2, 2).transpose(0, 4, 3, 2, 5, 1)  5.94 us
    convert_element_type x1, local copies, waits for them, and re-layouts, on_device(): (blocks[:, :, None, :, None] * both[None, None, :, None, :]).reshape(11 *...  5.26 us
    reshape x1, local copies, waits for them, and re-layouts, on_device(): turned = turned.reshape(LOCAL, 2, PAIRS, WIDTH, 128)  4.56 us
    convert_element_type x1, other arithmetic, on_device(): (blocks[:, :, None, :, None] * both[None, None, :, None, :]).reshape(11 *...  3 us
    ppermute x1, starting transfers between devices, on_device(): before = lax.ppermute(turned[:, :, :, 8:], 'tile', up)  2.69 us
  transfers between devices with their start and end apart: 2, of which 1 were waited for; matrix products, arithmetic and copies ran while one was open for 7% of the time, Pallas kernels for 0%

profile of v1, /device:TPU:1, one launch (start us, length us, event | category | flops | bytes accessed | tf_op | source)
XLA Modules:
  0.0 129.6 jit_solution(15790397352062893628)
XLA Ops:
  0.6 0.0 copy-start
  0.6 5.1 %copy.12 = bf16[5,64,16,128]{1,2,3,0:T(8,128)(2,1)} copy(bf16[5,64,16,128]{3,2,1,0:T(8,128)(2,1)} %param.10) | data formatting | bytes 2621440 | tf_op args[2]
  5.7 5.9 %copy.13 = bf16[5,2,32,16,2,64]{5,4,3,2,1,0:T(2,128)(2,1)} copy(bf16[5,2,32,16,2,64]{5,3,4,1,2,0:T(8,128)(2,1)} %bitcast.5) | data formatting | bytes 2621440 | tf_op jit(solution)/shard_map/transpose | solution.py:453
  11.7 0.0 copy-start.3
  11.7 0.0 copy-start.2
  11.7 4.6 %reshape.18 = bf16[5,2,32,16,128]{4,3,2,1,0:T(8,128)(2,1)S(1)} reshape(bf16[5,2,32,16,2,64]{5,4,3,2,1,0:T(2,128)(2,1)} %copy.13) | data formatting | bytes 2621440 | tf_op jit(solution)/shard_map/reshape | solution.py:454
  16.2 1.2 fusion
  17.4 2.7 %collective-permute-start = (bf16[5,2,32,8,128]{4,3,2,1,0:T(8,128)(2,1)}, bf16[5,2,32,8,128]{4,3,2,1,0:T(8,128)(2,1)S(1)}, u32[]{:S(2)}, u32[]{:S(2)}) collective-permute-start(bf16[5,2,32,8,128]{4,3,2,1,0:T(8,128)(2,1)} %get-tuple-element.2), channel_id=1, source_target_pairs={{0,4},{4,8},{8,12},{12,16},{16,20},{20,24},{24,28},{28,32},{32,36}... | collective-permute-start | bytes 1966088 | tf_op jit(solution)/shard_map/ppermute | solution.py:457
  20.1 0.6 collective-permute-start.1
  20.7 0.0 copy-done.3
  20.7 0.7 copy.14.st_ref
  21.3 0.0 copy-done
  21.3 0.2 convolution_multiply_fusion
  21.5 0.0 copy-done.2
  21.5 3.0 %multiply_convert_fusion = bf16[11,4,64,4,64]{4,3,2,1,0:T(4,128)(2,1)} fusion(f32[64,64]{1,0:T(8,128)S(1)} %convolution_multiply_fusion, f32[11,4,4]{2,1,0:T(4,128)S(1)} %copy-done.2), kind=kLoop, calls=%fused_computation | loop fusion | flops 1441792 | bytes 1458880 | tf_op jit(solution)/shard_map/convert_element_type | solution.py:463
  24.5 5.3 %convert_element_type.6.amat_hbm = bf16[2816,256]{1,0:T(8,128)(2,1)} reshape(bf16[11,4,64,4,64]{4,3,2,1,0:T(4,128)(2,1)} %multiply_convert_fusion) | data formatting | bytes 2883584 | tf_op jit(solution)/shard_map/convert_element_type | solution.py:463
  29.8 0.0 collective-permute-done
  29.8 0.6 collective-permute-done.1
  30.4 2.0 %pad_maximum_fusion.mem_hbm = bf16[5,2,32,32,128]{4,3,2,1,0:T(8,128)(2,1)} fusion(bf16[5,2,32,8,128]{4,3,2,1,0:T(8,128)(2,1)S(1)} %collective-permute-done.1, bf16[5,2,32,8,128]{4,3,2,1,0:T(8,128)(2,1)S(1)} %collective-permute-done, bf16[5,2,32,16,128]{4,3,2,1,0:T(8,128)(2,1)S(1)} %reshape.18), kind=kLoop, calls=%fused_computation.1 | loop fusion | flops 7864320 | bytes 5242880 | tf_op jit(solution)/shard_map/concatenate | solution.py:459
  32.4 92.5 %conjugate_gradient.1 = (f32[64,4,2048]{2,1,0:T(4,128)}, f32[64,4,2048]{2,1,0:T(4,128)}) custom-call(f32[64,4,2048]{2,1,0:T(4,128)} %b_hbm.1, f32[64,4,2048]{2,1,0:T(4,128)} %s_hbm.1, bf16[5,2,32,32,128]{4,3,2,1,0:T(8,128)(2,1)} %pad_maximum_fusion.mem_hbm, bf16[2816,256]{1,0:T(8,128)(2,1)} %convert_element_type.6.amat_hbm, ...), custom_call_target="tpu_custom_call" | custom-call | tf_op jit(solution)/shard_map/conjugate_gradient/pallas_call | solution.py:467
  124.9 0.0 copy-start.1
  124.9 3.3 %copy.17 = f32[64,4,2048]{2,1,0:T(4,128)} copy(f32[64,4,2048]{2,1,0:T(4,128)} %get-tuple-element.6) | data formatting | bytes 4194304
  128.3 0.0 copy-done.1
  128.3 1.3 %copy.18 = f32[64,4,2048]{2,1,0:T(4,128)} copy(f32[64,4,2048]{2,1,0:T(4,128)S(1)} %copy-done.1) | data formatting | bytes 4194304
Async XLA Ops:
  0.6 20.7 %copy-start = (f32[64,64]{1,0:T(8,128)S(1)}, f32[64,64]{1,0:T(8,128)}, u32[]{:S(2)}) copy-start(f32[64,64]{1,0:T(8,128)} %param.11) | copy-start | bytes 49156
  11.7 9.0 %copy-start.3 = (s32[8,4]{0,1:T(4,128)S(1)}, s32[8,4]{0,1:T(4,128)}, u32[]{:S(2)}) copy-start(s32[8,4]{0,1:T(4,128)} %param.12) | copy-start | bytes 388
  11.7 9.9 %copy-start.2 = (f32[11,4,4]{2,1,0:T(4,128)S(1)}, f32[11,4,4]{2,1,0:T(4,128)}, u32[]{:S(2)}) copy-start(f32[11,4,4]{2,1,0:T(4,128)} %constant.7.clone) | copy-start | bytes 2116
  17.4 12.4 %collective-permute-start = (bf16[5,2,32,8,128]{4,3,2,1,0:T(8,128)(2,1)}, bf16[5,2,32,8,128]{4,3,2,1,0:T(8,128)(2,1)S(1)}, u32[]{:S(2)}, u32[]{:S(2)}) collective-permute-start(bf16[5,2,32,8,128]{4,3,2,1,0:T(8,128)(2,1)} %get-tuple-element.2), channel_id=1, source_target_pairs={{0,4},{4,8},{8,12},{12,16},{16,20},{20,24},{24,28},{28,32},{32,36}... | collective-permute-start | bytes 1966088 | tf_op jit(solution)/shard_map/ppermute | solution.py:457
  20.1 10.3 %collective-permute-start.1 = (bf16[5,2,32,8,128]{4,3,2,1,0:T(8,128)(2,1)S(1)}, bf16[5,2,32,8,128]{4,3,2,1,0:T(8,128)(2,1)S(1)}, u32[]{:S(2)}, u32[]{:S(2)}) collective-permute-start(bf16[5,2,32,8,128]{4,3,2,1,0:T(8,128)(2,1)S(1)} %get-tuple-element.3), channel_id=1, source_target_pairs={{4,0},{8,4},{12,8},{16,12},{20,16},{24,20},{28,24},{32,28},{36,32}... | collective-permute-start | bytes 1966088 | tf_op jit(solution)/shard_map/ppermute | solution.py:458
  124.9 3.3 %copy-start.1 = (f32[64,4,2048]{2,1,0:T(4,128)S(1)}, f32[64,4,2048]{2,1,0:T(4,128)}, u32[]{:S(2)}) copy-start(f32[64,4,2048]{2,1,0:T(4,128)} %get-tuple-element.7) | copy-start | bytes 6291460

commit v2 on v1

--- a/solution.py
+++ b/solution.py
@@ -66,13 +66,16 @@
 
 
 def kernel(
-    b_hbm, s_hbm, mem_hbm, amat_hbm, xop_hbm, st_ref, w_hbm, sol_hbm, res_hbm,
-    bv, sv, ab, mem, amat, xop, wv, fb, onehot, send_c, recv_c, own_c, u, ens, es, rs, zs, back, hs, outv,
+    b_hbm, s_hbm, mem_hbm, root_ref, coef_ref, xop, perm, st_ref, w_hbm, sol_hbm, res_hbm,
+    bv, sv, ab, mraw, wide_t, wide_g, halo_send, halo_recv, mem, amat, wv, fb, onehot, send_c, recv_c, own_c, u, ens, es, rs, zs, back, hs, outv,
     part, sc1, sc2, sc3,
-    load_sem, a_send, a_recv, b_send, b_recv, c_send, c_recv, s_send, s_recv, out_sem,
+    load_sem, a_send, a_recv, b_send, b_recv, c_send, c_recv, s_send, s_recv, h_send, h_recv, out_sem,
 ):
     me = lax.axis_index("tile")
     mm = lax.axis_index("mem")
+
+    def wait_bytes(ref, sem):
+        pltpu.make_async_copy(ref, ref, sem).wait()
 
     def at_tile(t):
         return {"tile": t, "mem": mm}
@@ -96,33 +99,84 @@
     loads.append(pltpu.make_async_copy(w_hbm, wv, load_sem.at[4]))
     for r in range(4):
         loads.append(pltpu.make_async_copy(s_hbm.at[:, r, :], sv.at[r], load_sem.at[5 + r]))
-    loads.append(pltpu.make_async_copy(mem_hbm, mem, load_sem.at[9]))
-    loads.append(pltpu.make_async_copy(amat_hbm, amat, load_sem.at[10]))
-    loads.append(pltpu.make_async_copy(xop_hbm, xop, load_sem.at[11]))
+    loads.append(pltpu.make_async_copy(mem_hbm, mraw, load_sem.at[9]))
     for load in loads:
         load.start()
 
-    rows_at = lax.broadcasted_iota(jnp.int32, (LEV, 2 * LEV), 0)
-    lanes_at = lax.broadcasted_iota(jnp.int32, (LEV, 2 * LEV), 1)
-    eye0 = (lanes_at == rows_at).astype(F32)
-    eye1 = (lanes_at == rows_at + LEV).astype(F32)
-    for s in range(STENCIL):
-        for q in range(4):
-            e0 = st_ref[q, s]
-            e1 = st_ref[4 + q, s]
-
-            def place(j, carry, s=s, q=q, e0=e0, e1=e1):
-                h0 = jnp.where(e0 == j, 1.0, 0.0).astype(F32)
-                h1 = jnp.where(e1 == j, 1.0, 0.0).astype(F32)
-                onehot[pl.ds(pl.multiple_of((s * 8 + j) * LEV, LEV), LEV), q * 128 : q * 128 + 128] = (
-                    eye0 * h0 + eye1 * h1
-                ).astype(BF16)
-                return carry
-
-            lax.fori_loop(0, 8, place, 0)
-    for m in range(LOCAL):
-        u[m, 0:32, :] = jnp.zeros((32, 256), BF16)
-        u[m, 544:576, :] = jnp.zeros((32, 256), BF16)
+    def build():
+        rows_at = lax.broadcasted_iota(jnp.int32, (LEV, 2 * LEV), 0)
+        lanes_at = lax.broadcasted_iota(jnp.int32, (LEV, 2 * LEV), 1)
+        eye0 = (lanes_at == rows_at).astype(F32)
+        eye1 = (lanes_at == rows_at + LEV).astype(F32)
+        for s in range(STENCIL):
+            for q in range(4):
+                e0 = st_ref[q, s]
+                e1 = st_ref[4 + q, s]
+
+                def place(j, carry, s=s, q=q, e0=e0, e1=e1):
+                    h0 = jnp.where(e0 == j, 1.0, 0.0).astype(F32)
+                    h1 = jnp.where(e1 == j, 1.0, 0.0).astype(F32)
+                    onehot[pl.ds(pl.multiple_of((s * 8 + j) * LEV, LEV), LEV), q * 128 : q * 128 + 128] = (
+                        eye0 * h0 + eye1 * h1
+                    ).astype(BF16)
+                    return carry
+
+                lax.fori_loop(0, 8, place, 0)
+        for m in range(LOCAL):
+            u[m, 0:32, :] = jnp.zeros((32, 256), BF16)
+            u[m, 544:576, :] = jnp.zeros((32, 256), BF16)
+        both = lax.dot_general(
+            root_ref[...],
+            root_ref[...],
+            (((1,), (1,)), ((), ())),
+            preferred_element_type=F32,
+            precision=lax.Precision.HIGHEST,
+        ) * (1.0 / (MEMBERS - 1))
+        four = jnp.concatenate([both] * 4, axis=1)
+
+        def scale(n, carry):
+            amat[pl.ds(pl.multiple_of(n * LEV, LEV), LEV), :] = (four * coef_ref[pl.ds(n, 1), :]).astype(BF16)
+            return carry
+
+        lax.fori_loop(0, 44, scale, 0)
+
+    def halo_copy(side, m):
+        to = lax.rem(me + (TILES - 1 if side == 0 else 1), TILES)
+        return pltpu.make_async_remote_copy(
+            src_ref=halo_send.at[side, m],
+            dst_ref=halo_recv.at[side, m],
+            send_sem=h_send.at[side],
+            recv_sem=h_recv.at[side],
+            device_id=at_tile(to),
+            device_id_type=MESH,
+        )
+
+    def turn(m, carry):
+        wide_t[...] = mraw[m].reshape(COLS, 128).astype(F32)
+        for c in range(WIDTH):
+            at = wide_t[pl.ds(c, LEV, stride=WIDTH), :].astype(BF16)
+            rows = lax.dot_general(perm[...], at, (((1,), (1,)), ((), ())), preferred_element_type=F32)
+            wide_g[pl.ds(c, TILES, stride=WIDTH), :] = jnp.concatenate([rows[:64], rows[64:]], axis=1)
+        turned = wide_g[...]
+        mem[m, :, 0:16, :] = turned.reshape(TILES, 16, 128).astype(BF16)
+        halves = turned.reshape(TILES, 2, 8, 128)
+        for side in range(2):
+            halo_send[side, m] = halves[:, side].reshape(PAIRS, 16, 128).astype(BF16)
+            halo_copy(side, m).start()
+        return carry
+
+    def wait_halo():
+        for side in range(2):
+            wait_bytes(halo_recv.at[side], h_recv.at[side])
+            wait_bytes(halo_send.at[side], h_send.at[side])
+
+        def join(m, carry):
+            before = halo_recv[1, m].astype(F32).reshape(TILES, 8, 128)
+            after = halo_recv[0, m].astype(F32).reshape(TILES, 8, 128)
+            mem[m, :, 16:32, :] = jnp.concatenate([before, after], axis=1).astype(BF16)
+            return carry
+
+        lax.fori_loop(0, LOCAL, join, 0)
 
     def pack_row(v):
         return jnp.sum(v.reshape(-1, 8, 128), axis=0).sum(axis=0, keepdims=True)
@@ -153,8 +207,6 @@
 
     mine = lax.rem(me, 2) * PAIRS + lax.div(me, 2)
 
-    def wait_bytes(ref, sem):
-        pltpu.make_async_copy(ref, ref, sem).wait()
 
     def c_copy(it, t):
         return pltpu.make_async_remote_copy(
@@ -229,36 +281,82 @@
     def pick(tile, row):
         return jnp.sum(tile[row : row + 1, :], axis=1, keepdims=True)
 
-    def ensemble(it):
+    def mix(it):
         def member(m, carry):
             for g in range(4):
                 lanes = []
                 for par in range(2):
-                    w = mem[m, par, 8 * g : 8 * g + 8] * recv_c[it, par * PAIRS + 8 * g : par * PAIRS + 8 * g + 8]
-                    lanes.append(w.reshape(256, 128))
+                    at = par * PAIRS + 8 * g
+                    lanes.append((mem[m, at : at + 8] * recv_c[it, at : at + 8]).reshape(256, 128))
                 mixed = jnp.dot(xop[...], jnp.concatenate(lanes, axis=1), preferred_element_type=F32)
                 u[m, 32 + 128 * g : 160 + 128 * g, :] = mixed.astype(BF16)
-            for g in range(4):
-                at = 32 + 128 * g
-                wide = jnp.concatenate([u[m, at + 16 * d : at + 16 * d + 128, :] for d in range(-2, 3)], axis=1)
-                inner = jnp.dot(wide, amat[0:1280, :], preferred_element_type=F32)
-                if g == 0:
-                    edge = jnp.concatenate([u[m, 32 + 16 * d : 48 + 16 * d, :] for d in range(0, 3)], axis=1)
-                    edge = jnp.dot(edge, amat[1280:2048, :], preferred_element_type=F32)
-                    inner = jnp.concatenate([edge, inner[16:]], axis=0)
-                if g == 3:
-                    edge = jnp.concatenate([u[m, 528 + 16 * d : 544 + 16 * d, :] for d in range(-2, 1)], axis=1)
-                    edge = jnp.dot(edge, amat[2048:2816, :], preferred_element_type=F32)
-                    inner = jnp.concatenate([inner[:112], edge], axis=0)
+            return carry
+
+        lax.fori_loop(0, LOCAL, member, 0)
+
+    def own_part(m, at, count):
+        return mem[m, pl.ds(at, count), 0:16, :].astype(F32)
+
+    def ensemble(it):
+        mix(it)
+
+        def group(turn_at, carry):
+            k = jnp.where(turn_at == 0, 2, jnp.where(turn_at == 1, 1, jnp.where(turn_at == 2, 3, 0)))
+            g = lax.rem(mm + k, MEMS)
+            wide = []
+            for m in range(LOCAL):
+                pieces = []
+                for d in range(-2, 3):
+                    pieces.append(u[m, pl.ds(pl.multiple_of(32 + 128 * g + 16 * d, 16), 128), :])
+                wide.append(jnp.concatenate(pieces, axis=1))
+            inner = jnp.dot(jnp.concatenate(wide, axis=0), amat[0:1280, :], preferred_element_type=F32)
+            for par in range(2):
+                total = jnp.zeros((8, 16, 128), F32)
+                for m in range(LOCAL):
+                    term = inner[m * 128 : m * 128 + 128, par * 128 : par * 128 + 128].reshape(8, 16, 128)
+                    total = total + own_part(m, par * PAIRS + 8 * g, 8) * term
+                ens[pl.ds(par * PAIRS + 8 * g, 8)] = total
+
+            def edge(pair, shifts, at):
+                wide = []
+                for m in range(LOCAL):
+                    wide.append(
+                        jnp.concatenate([u[m, 32 + 16 * (pair + d) : 48 + 16 * (pair + d), :] for d in shifts], axis=1)
+                    )
+                inner = jnp.dot(
+                    jnp.concatenate(wide, axis=0), amat[at : at + 768, :], preferred_element_type=F32
+                )
                 for par in range(2):
-                    own = mem[m, par, 8 * g : 8 * g + 8, 0:16, :].astype(F32)
-                    term = own * inner[:, par * 128 : par * 128 + 128].reshape(8, 16, 128)
-                    ens[par, 8 * g : 8 * g + 8] += term
+                    total = jnp.zeros((1, 16, 128), F32)
+                    for m in range(LOCAL):
+                        term = inner[m * 16 : m * 16 + 16, par * 128 : par * 128 + 128].reshape(1, 16, 128)
+                        total = total + own_part(m, par * PAIRS + pair, 1) * term
+                    ens[par * PAIRS + pair : par * PAIRS + pair + 1] = total
+
+            @pl.when(g == 0)
+            def _():
+                edge(0, range(0, 3), 1280)
+
+            @pl.when(g == 3)
+            def _():
+                edge(PAIRS - 1, range(-2, 1), 2048)
+
+            even = ens[pl.ds(8 * g, 8)]
+            odd = ens[pl.ds(PAIRS + 8 * g, 8)]
+            both = jnp.stack([even, odd], axis=1).reshape(QUARTER, 16, 128).astype(BF16)
+            es[it, pl.ds(g * QUARTER, QUARTER)] = both
+
+            @pl.when(turn_at < 3)
+            def _():
+                rs_copy(it, k).start()
+
+            @pl.when(turn_at == 3)
+            def _():
+                rs[it, mm] = both
+
             return carry
 
-        ens[...] = jnp.zeros_like(ens)
-        lax.fori_loop(0, LOCAL, member, 0)
-        es[it] = jnp.stack([ens[0], ens[1]], axis=1).reshape(TILES, 16, 128).astype(BF16)
+        lax.fori_loop(0, MEMS, group, 0)
 
     def rs_copy(it, k):
         to = lax.rem(mm + k, MEMS)
@@ -270,11 +368,6 @@
             device_id=at_mem(to),
             device_id_type=MESH,
         )
-
-    def start_rs(it):
-        for k in (2, 1, 3):
-            rs_copy(it, k).start()
-        rs[it, mm] = es[it, pl.ds(mm * QUARTER, QUARTER)]
 
     def wait_rs(it):
         wait_bytes(rs.at[it, 0 : MEMS - 1], b_recv.at[it])
@@ -348,6 +441,7 @@
         fill_blocks(r, bv[r].astype(BF16))
     loads[4].wait()
     restrict(0)
+    build()
     pl.semaphore_wait(barrier, TILES - 1 + MEMS - 1)
     start_c(0)
     for r in range(4):
@@ -359,19 +453,16 @@
         square = square + pack_row(v * v)
         diag = diag + pack_row(v * v * (1.0 + sv[r]))
     sum_start(0, 0, stack_rows([square, diag]))
-    for load in loads[9:]:
-        load.wait()
+    loads[9].wait()
+    lax.fori_loop(0, LOCAL, turn, 0)
     sum_start(0, 1, sum_end(0, 0))
     first_sums = sum_end(0, 1)
+    wait_halo()
     wait_c(0)
     ensemble(0)
-    start_rs(0)
 
     def col_dot(c_it):
-        v = jnp.zeros((1, 128), F32)
-        for par in range(2):
-            v = v + pack_row(ens[par] * recv_c[c_it, par * PAIRS : par * PAIRS + PAIRS, 0:16, :].astype(F32))
-        return v
+        return pack_row(ens[...] * recv_c[c_it, :, 0:16, :].astype(F32))
 
     sum_start(1, 0, stack_rows([col_dot(0)]))
     wait_rs(0)
@@ -411,7 +502,6 @@
     third_sums = sum_end(2, 1)
     wait_c(1)
     ensemble(1)
-    start_rs(1)
     sum_start(3, 0, stack_rows([col_dot(1), col_dot(0)]))
     wait_rs(1)
     start_back(1)
@@ -425,6 +515,7 @@
     alpha2 = new / dad2
     wait_back(1)
     gather_back(1)
+    stores = []
     for piece in range(4):
         rr_, half = piece // 2, piece % 2
         total = prolong(piece)
@@ -439,43 +530,45 @@
                 second = rnew * (1.0 + sv[r, :, cols]) + total[j * 64 : j * 64 + 64, :] + beta * image
                 outv[0, r, :, cols] = alpha * d + alpha2 * (rnew + beta * d)
                 outv[1, r, :, cols] = rnew - alpha2 * second
-    stores = []
-    for r in range(4):
-        stores.append(pltpu.make_async_copy(outv.at[0, r], sol_hbm.at[:, r, :], out_sem.at[r]))
-        stores.append(pltpu.make_async_copy(outv.at[1, r], res_hbm.at[:, r, :], out_sem.at[4 + r]))
-    for store in stores:
-        store.start()
+        if half == 1:
+            for r in (rr_, 2 + rr_):
+                stores.append(pltpu.make_async_copy(outv.at[0, r], sol_hbm.at[:, r, :], out_sem.at[r]))
+                stores.append(pltpu.make_async_copy(outv.at[1, r], res_hbm.at[:, r, :], out_sem.at[4 + r]))
+                stores[-2].start()
+                stores[-1].start()
     for store in stores:
         store.wait()
 
 
 def on_device(right_side, static_var, members, vertical_root, stencil, weights):
-    turned = members.reshape(LOCAL, LEV, WIDTH, PAIRS, 2, 2).transpose(0, 4, 3, 2, 5, 1)
-    turned = turned.reshape(LOCAL, 2, PAIRS, WIDTH, 128)
-    up = [(i, (i + 1) % TILES) for i in range(TILES)]
-    down = [(j, i) for i, j in up]
-    before = lax.ppermute(turned[:, :, :, 8:], "tile", up)
-    after = lax.ppermute(turned[:, :, :, :8], "tile", down)
-    extended = jnp.concatenate([turned, before, after], axis=3)
-    both = jnp.einsum("kl,jl->kj", vertical_root, vertical_root, precision=lax.Precision.HIGHEST)
-    both = both / (MEMBERS - 1)
-    blocks = jnp.asarray(row_blocks(), F32)
-    amat = (blocks[:, :, None, :, None] * both[None, None, :, None, :]).reshape(11 * 256, 256).astype(BF16)
+    coef = np.repeat(row_blocks().reshape(44, 4), LEV, axis=1)
+    coef = jnp.asarray(np.concatenate([coef, np.zeros((4, 256))]), F32)
+    order = np.zeros((ROWS, ROWS))
+    for i in range(2):
+        for par in range(2):
+            for pair in range(PAIRS):
+                order[i * 64 + par * PAIRS + pair, 4 * pair + 2 * par + i] = 1.0
+    perm = jnp.asarray(order, BF16)
     xop = jnp.asarray(column_operator(), BF16)
+    vmem = pl.BlockSpec(memory_space=pltpu.VMEM)
     anyspec = pl.BlockSpec(memory_space=pl.ANY)
     field = jax.ShapeDtypeStruct(right_side.shape, F32)
     return pl.pallas_call(
         kernel,
         out_shape=(field, field),
-        in_specs=[anyspec] * 5 + [pl.BlockSpec(memory_space=pltpu.SMEM), anyspec],
+        in_specs=[anyspec] * 3 + [vmem] * 4 + [pl.BlockSpec(memory_space=pltpu.SMEM), anyspec],
         out_specs=(anyspec, anyspec),
         scratch_shapes=[
             pltpu.VMEM((4, LEV, 2048), F32),
             pltpu.VMEM((4, LEV, 2048), F32),
             pltpu.VMEM((4, LEV, 2048), F32),
-            pltpu.VMEM((LOCAL, 2, PAIRS, 32, 128), BF16),
+            pltpu.VMEM((LOCAL, LEV, WIDTH, 128), BF16),
+            pltpu.VMEM((COLS, 128), F32),
+            pltpu.VMEM((COLS, 128), F32),
+            pltpu.VMEM((2, LOCAL, PAIRS, 16, 128), BF16),
+            pltpu.VMEM((2, LOCAL, PAIRS, 16, 128), BF16),
+            pltpu.VMEM((LOCAL, TILES, 32, 128), BF16),
             pltpu.VMEM((11 * 256, 256), BF16),
-            pltpu.VMEM((128, 256), BF16),
             pltpu.VMEM((STENCIL, 1024, 256), BF16),
             pltpu.VMEM((8, LEV, 1024), BF16),
             pltpu.VMEM((2048, 512), BF16),
@@ -483,7 +576,7 @@
             pltpu.VMEM((2, TILES, 32, 128), BF16),
             pltpu.VMEM((COLS, 128), F32),
             pltpu.VMEM((LOCAL, 576, 256), BF16),
-            pltpu.VMEM((2, PAIRS, 16, 128), F32),
+            pltpu.VMEM((TILES, 16, 128), F32),
             pltpu.VMEM((2, TILES, 16, 128), BF16),
             pltpu.VMEM((2, MEMS, QUARTER, 16, 128), BF16),
             pltpu.VMEM((2, QUARTER, 16, 128), BF16),
@@ -503,13 +596,15 @@
             pltpu.SemaphoreType.DMA((2,)),
             pltpu.SemaphoreType.DMA((4, 3)),
             pltpu.SemaphoreType.DMA((4, 3)),
+            pltpu.SemaphoreType.DMA((2,)),
+            pltpu.SemaphoreType.DMA((2,)),
             pltpu.SemaphoreType.DMA((8,)),
         ],
         compiler_params=pltpu.CompilerParams(
-            collective_id=0, has_side_effects=True, vmem_limit_bytes=56 * 1024 * 1024
+            collective_id=0, has_side_effects=True, vmem_limit_bytes=58 * 1024 * 1024
         ),
         name="conjugate_gradient",
-    )(right_side, static_var, extended, amat, xop, stencil, weights)
+    )(right_side, static_var, members, vertical_root, coef, xop, perm, stencil, weights)
 
 
 def solution(mesh):

time: 132 us -> 108 us (0.82)
  local copies, waits for them, and re-layouts: 27.3 us -> 5.98 us
  Pallas kernels: 92.5 us -> 99.1 us
  other arithmetic: 4.98 us -> 0 us
  starting transfers between devices: 3.24 us -> 0 us
    pallas_call x1, Pallas kernels: 92.5 us -> 99.1 us  [on_device(): pl.pallas_call(kernel, out_shape=(field, field), in_specs=[anyspec] * 3 +...]
    transpose x1 -> x0, local copies, waits for them, and re-layouts: 5.94 us -> none  [on_device(): members.reshape(LOCAL, LEV, WIDTH, PAIRS, 2, 2).transpose(0, 4, 3, 2, 5, 1)]
    convert_element_type x1 -> x0, local copies, waits for them, and re-layouts: 5.26 us -> none  [on_device(): (blocks[:, :, None, :, None] * both[None, None, :, None, :]).reshape(11 *...]
    reshape x1 -> x0, local copies, waits for them, and re-layouts: 4.56 us -> none  [on_device(): turned = turned.reshape(LOCAL, 2, PAIRS, WIDTH, 128)]
    unnamed x12 -> x5, local copies, waits for them, and re-layouts: 10.4 us -> 5.98 us
    ppermute x2 -> x0, starting transfers between devices: 3.24 us -> none  [the longest x1 2.69 us: on_device(): before = lax.ppermute(turned[:, :, :, 8:], 'tile', up)]
    convert_element_type x1 -> x0, other arithmetic: 3 us -> none  [on_device(): (blocks[:, :, None, :, None] * both[None, None, :, None, :]).reshape(11 *...]
    concatenate x1 -> x0, other arithmetic: 1.98 us -> none  [on_device(): extended = jnp.concatenate([turned, before, after], axis=3)]
  transfers between devices with their start and end apart: 2 -> 0, of which waited for: 1 -> 0; matrix products, arithmetic and copies ran while one was open for 7% -> 0% of each run, Pallas kernels for 0% -> 0%
where the time goes in v2:
time: 108 us; the launch traced here: 106 us
  Pallas kernels  99.1 us (92%)
  local copies, waits for them, and re-layouts  5.98 us (6%)
    pallas_call x1, Pallas kernels, on_device(): pl.pallas_call(kernel, out_shape=(field, field), in_specs=[anyspec] * 3 +...  99.1 us
    unnamed x5, local copies, waits for them, and re-layouts  5.98 us

profile of v2, /device:TPU:1, one launch (start us, length us, event | category | flops | bytes accessed | tf_op | source)
XLA Modules:
  0.0 105.7 jit_solution(3497282380266654641)
XLA Ops:
  0.6 1.3 %copy.11.st_ref = s32[8,4]{1,0:T(8,128)} copy(s32[8,4]{0,1:T(4,128)} %param.13) | data formatting | bytes 256 | tf_op args[4]
  2.0 99.1 %conjugate_gradient.1 = (f32[64,4,2048]{2,1,0:T(4,128)}, f32[64,4,2048]{2,1,0:T(4,128)}) custom-call(f32[64,4,2048]{2,1,0:T(4,128)} %b_hbm.1, f32[64,4,2048]{2,1,0:T(4,128)} %s_hbm.1, bf16[5,64,16,128]{3,2,1,0:T(8,128)(2,1)} %mem_hbm.1, f32[64,64]{1,0:T(8,128)} %root_ref.1, f32[48,256]{1,0:T(8,128)} %constant.6.clone.coef_ref, ...), custom_call_target="tpu_custom_call" | custom-call | tf_op jit(solution)/shard_map/conjugate_gradient/pallas_call | solution.py:556
  101.0 0.0 copy-start
  101.1 3.3 %copy.14 = f32[64,4,2048]{2,1,0:T(4,128)} copy(f32[64,4,2048]{2,1,0:T(4,128)} %get-tuple-element.4) | data formatting | bytes 4194304
  104.4 0.0 copy-done
  104.4 1.3 %copy.15 = f32[64,4,2048]{2,1,0:T(4,128)} copy(f32[64,4,2048]{2,1,0:T(4,128)S(1)} %copy-done) | data formatting | bytes 4194304
Async XLA Ops:
  101.0 3.3 %copy-start = (f32[64,4,2048]{2,1,0:T(4,128)S(1)}, f32[64,4,2048]{2,1,0:T(4,128)}, u32[]{:S(2)}) copy-start(f32[64,4,2048]{2,1,0:T(4,128)} %get-tuple-element.5) | copy-start | bytes 6291460

commit v3 on v2

--- a/solution.py
+++ b/solution.py
@@ -69,7 +69,7 @@
     b_hbm, s_hbm, mem_hbm, root_ref, coef_ref, xop, perm, st_ref, w_hbm, sol_hbm, res_hbm,
     bv, sv, ab, mraw, wide_t, wide_g, halo_send, halo_recv, mem, amat, wv, fb, onehot, send_c, recv_c, own_c, u, ens, es, rs, zs, back, hs, outv,
     part, sc1, sc2, sc3,
-    load_sem, a_send, a_recv, b_send, b_recv, c_send, c_recv, s_send, s_recv, h_send, h_recv, out_sem,
+    load_sem, a_send, a_recv, b_send, b_recv, c_send, c_recv, s_send, s_recv, h_send, h_recv, ready, out_sem,
 ):
     me = lax.axis_index("tile")
     mm = lax.axis_index("mem")
@@ -100,7 +100,8 @@
     for r in range(4):
         loads.append(pltpu.make_async_copy(s_hbm.at[:, r, :], sv.at[r], load_sem.at[5 + r]))
     loads.append(pltpu.make_async_copy(mem_hbm, mraw, load_sem.at[9]))
-    for load in loads:
+    loads[9].start()
+    for load in loads[:9]:
         load.start()
 
     def build():
@@ -162,7 +163,6 @@
         halves = turned.reshape(TILES, 2, 8, 128)
         for side in range(2):
             halo_send[side, m] = halves[:, side].reshape(PAIRS, 16, 128).astype(BF16)
-            halo_copy(side, m).start()
         return carry
 
     def wait_halo():
@@ -205,6 +205,7 @@
         for q in range(4):
             fb[4 * p + q, :, rr * 512 : rr * 512 + 512] = field[:, q * 512 : q * 512 + 512]
 
+    group_of_me = lax.div(me, QUARTER)
     mine = lax.rem(me, 2) * PAIRS + lax.div(me, 2)
 
 
@@ -213,7 +214,7 @@
             src_ref=send_c.at[it, t],
             dst_ref=recv_c.at[it, mine],
             send_sem=a_send.at[it],
-            recv_sem=a_recv.at[it],
+            recv_sem=a_recv.at[it, group_of_me],
             device_id=at_tile(t),
             device_id_type=MESH,
         )
@@ -224,10 +225,9 @@
             return carry
 
         lax.fori_loop(1, TILES, go, 0)
-        recv_c[it, mine] = send_c[it, me]
+        pltpu.make_async_copy(send_c.at[it, me], recv_c.at[it, mine], a_recv.at[it, group_of_me]).start()
 
     def wait_c(it):
-        wait_bytes(recv_c.at[it, 0 : TILES - 1], a_recv.at[it])
         wait_bytes(send_c.at[it, 0 : TILES - 1], a_send.at[it])
 
     low = lax.rem(me, 8)
@@ -282,27 +282,50 @@
         return jnp.sum(tile[row : row + 1, :], axis=1, keepdims=True)
 
     def mix(it):
-        def member(m, carry):
-            for g in range(4):
+        def group(turn_at, carry):
+            g = lax.rem(group_of_me + 3 - turn_at, 4)
+            wait_bytes(recv_c.at[it, 0:QUARTER], a_recv.at[it, g])
+            for m in range(LOCAL):
                 lanes = []
                 for par in range(2):
                     at = par * PAIRS + 8 * g
-                    lanes.append((mem[m, at : at + 8] * recv_c[it, at : at + 8]).reshape(256, 128))
+                    lanes.append((mem[m, pl.ds(at, 8)] * recv_c[it, pl.ds(at, 8)]).reshape(256, 128))
                 mixed = jnp.dot(xop[...], jnp.concatenate(lanes, axis=1), preferred_element_type=F32)
-                u[m, 32 + 128 * g : 160 + 128 * g, :] = mixed.astype(BF16)
+                u[m, pl.ds(pl.multiple_of(32 + 128 * g, 32), 128), :] = mixed.astype(BF16)
             return carry
 
-        lax.fori_loop(0, LOCAL, member, 0)
+        lax.fori_loop(0, 4, group, 0)
 
     def own_part(m, at, count):
         return mem[m, pl.ds(at, count), 0:16, :].astype(F32)
 
+    to_self = lax.rem(group_of_me + me, MEMS) == mm
+    segment = lax.rem(mm + TILES - me, MEMS)
+    slot = lax.rem(me, QUARTER)
+
+    def out_go(it, t):
+        itself = jnp.logical_and(t == me, to_self)
+
+        @pl.when(jnp.logical_not(itself))
+        def _():
+            pltpu.make_async_remote_copy(
+                src_ref=es.at[it, t],
+                dst_ref=rs.at[it, mm, slot],
+                send_sem=b_send.at[it],
+                recv_sem=b_recv.at[it],
+                device_id={"tile": t, "mem": lax.rem(group_of_me + t, MEMS)},
+                device_id_type=MESH,
+            ).start()
+
+        @pl.when(itself)
+        def _():
+            pltpu.make_async_copy(es.at[it, t], rs.at[it, mm, slot], b_recv.at[it]).start()
+
     def ensemble(it):
         mix(it)
 
         def group(turn_at, carry):
-            k = jnp.where(turn_at == 0, 2, jnp.where(turn_at == 1, 1, jnp.where(turn_at == 2, 3, 0)))
-            g = lax.rem(mm + k, MEMS)
+            g = lax.rem(me + mm + turn_at, 4)
             wide = []
             for m in range(LOCAL):
                 pieces = []
@@ -346,76 +369,49 @@
             both = jnp.stack([even, odd], axis=1).reshape(QUARTER, 16, 128).astype(BF16)
             es[it, pl.ds(g * QUARTER, QUARTER)] = both
 
-            @pl.when(turn_at < 3)
-            def _():
-                rs_copy(it, k).start()
-
-            @pl.when(turn_at == 3)
-            def _():
-                rs[it, mm] = both
-
+            def go(k, inner_carry):
+                out_go(it, g * QUARTER + lax.rem(me + k, QUARTER))
+                return inner_carry
+
+            lax.fori_loop(0, QUARTER, go, 0)
             return carry
 
         lax.fori_loop(0, MEMS, group, 0)
 
-    def rs_copy(it, k):
-        to = lax.rem(mm + k, MEMS)
-        return pltpu.make_async_remote_copy(
-            src_ref=es.at[it, pl.ds(to * QUARTER, QUARTER)],
-            dst_ref=rs.at[it, mm],
-            send_sem=b_send.at[it],
-            recv_sem=b_recv.at[it],
-            device_id=at_mem(to),
-            device_id_type=MESH,
-        )
-
     def wait_rs(it):
-        wait_bytes(rs.at[it, 0 : MEMS - 1], b_recv.at[it])
-        wait_bytes(rs.at[it, 0 : MEMS - 1], b_send.at[it])
+        wait_bytes(es.at[it], b_recv.at[it])
+
+        @pl.when(to_self)
+        def _():
+            wait_bytes(es.at[it, 0 : TILES - 1], b_send.at[it])
+
+        @pl.when(jnp.logical_not(to_self))
+        def _():
+            wait_bytes(es.at[it], b_send.at[it])
+
         total = rs[it, 0].astype(F32)
         for m in range(1, MEMS):
             total = total + rs[it, m].astype(F32)
         zs[it] = total.astype(BF16)
 
-    def back_copy(it, tt, m):
+    def back_copy(it, k):
         return pltpu.make_async_remote_copy(
-            src_ref=zs.at[it, tt],
-            dst_ref=back.at[it, me],
+            src_ref=zs.at[it],
+            dst_ref=back.at[it, pl.ds(segment * QUARTER, QUARTER)],
             send_sem=c_send.at[it],
             recv_sem=c_recv.at[it],
-            device_id={"tile": mm * QUARTER + tt, "mem": m},
+            device_id=at_mem(lax.rem(mm + k, MEMS)),
             device_id_type=MESH,
         )
 
     def start_back(it):
-        def go(k, carry):
-            m = lax.rem(mm + lax.div(k, QUARTER), MEMS)
-            tt = lax.rem(me + k, QUARTER)
-            itself = jnp.logical_and(mm * QUARTER + tt == me, m == mm)
-
-            @pl.when(jnp.logical_not(itself))
-            def _():
-                back_copy(it, tt, m).start()
-
-            @pl.when(itself)
-            def _():
-                pltpu.make_async_copy(zs.at[it, tt], back.at[it, me], c_recv.at[it]).start()
-
-            return carry
-
-        lax.fori_loop(0, TILES, go, 0)
+        for k in (2, 1, 3):
+            back_copy(it, k).start()
+        back[it, pl.ds(segment * QUARTER, QUARTER)] = zs[it]
 
     def wait_back(it):
-        wait_bytes(back.at[it], c_recv.at[it])
-        to_self = lax.div(me, QUARTER) == mm
-
-        @pl.when(to_self)
-        def _():
-            wait_bytes(back.at[it, 0 : TILES - 1], c_send.at[it])
-
-        @pl.when(jnp.logical_not(to_self))
-        def _():
-            wait_bytes(back.at[it], c_send.at[it])
+        wait_bytes(back.at[it, 0 : 3 * QUARTER], c_recv.at[it])
+        wait_bytes(back.at[it, 0 : 3 * QUARTER], c_send.at[it])
 
     def gather_back(it):
         wide = jnp.concatenate([back[it, 16 * q : 16 * q + 16].reshape(256, 128) for q in range(4)], axis=1)
@@ -436,13 +432,23 @@
             total = term if total is None else total + term
         return total
 
+    loads[9].wait()
+    lax.fori_loop(0, LOCAL, turn, 0)
+    pl.semaphore_wait(barrier, TILES - 1 + MEMS - 1)
+
+    def send_halo(m, carry):
+        halo_copy(0, m).start()
+        halo_copy(1, m).start()
+        return carry
+
+    lax.fori_loop(0, LOCAL, send_halo, 0)
+    for k in range(1, MEMS):
+        pl.semaphore_signal(ready, inc=1, device_id=at_mem(lax.rem(mm + k, MEMS)), device_id_type=MESH)
     for r in range(4):
         loads[r].wait()
         fill_blocks(r, bv[r].astype(BF16))
     loads[4].wait()
     restrict(0)
-    build()
-    pl.semaphore_wait(barrier, TILES - 1 + MEMS - 1)
     start_c(0)
     for r in range(4):
         loads[5 + r].wait()
@@ -453,22 +459,22 @@
         square = square + pack_row(v * v)
         diag = diag + pack_row(v * v * (1.0 + sv[r]))
     sum_start(0, 0, stack_rows([square, diag]))
-    loads[9].wait()
-    lax.fori_loop(0, LOCAL, turn, 0)
+    build()
+    wait_halo()
     sum_start(0, 1, sum_end(0, 0))
-    first_sums = sum_end(0, 1)
-    wait_halo()
-    wait_c(0)
+    pl.semaphore_wait(ready, MEMS - 1)
     ensemble(0)
 
     def col_dot(c_it):
         return pack_row(ens[...] * recv_c[c_it, :, 0:16, :].astype(F32))
 
     sum_start(1, 0, stack_rows([col_dot(0)]))
+    wait_c(0)
+    first_sums = sum_end(0, 1)
+    sum_start(1, 1, sum_end(1, 0))
     wait_rs(0)
+    sum_start(1, 2, sum_end(1, 1))
     start_back(0)
-    sum_start(1, 1, sum_end(1, 0))
-    sum_start(1, 2, sum_end(1, 1))
     second_sums = sum_end(1, 2)
     rr = pick(first_sums, 0)
     dad = pick(first_sums, 1) + pick(second_sums, 0)
@@ -495,18 +501,18 @@
                 square = square + pack_row(rnew * rnew)
                 diag = diag + pack_row(rnew * rnew * factor)
                 cross = cross + pack_row(d * rnew * factor)
+    sum_start(2, 0, stack_rows([square, diag, cross]))
     restrict(1)
+    sum_start(2, 1, sum_end(2, 0))
     start_c(1)
-    sum_start(2, 0, stack_rows([square, diag, cross]))
-    sum_start(2, 1, sum_end(2, 0))
-    third_sums = sum_end(2, 1)
-    wait_c(1)
     ensemble(1)
     sum_start(3, 0, stack_rows([col_dot(1), col_dot(0)]))
+    wait_c(1)
+    third_sums = sum_end(2, 1)
+    sum_start(3, 1, sum_end(3, 0))
     wait_rs(1)
+    sum_start(3, 2, sum_end(3, 1))
     start_back(1)
-    sum_start(3, 1, sum_end(3, 0))
-    sum_start(3, 2, sum_end(3, 1))
     fourth_sums = sum_end(3, 2)
     new = pick(third_sums, 0)
     beta = new / rr
@@ -589,7 +595,7 @@
             pltpu.VMEM((4, MEMS, 8, 128), F32),
             pltpu.SemaphoreType.DMA((12,)),
             pltpu.SemaphoreType.DMA((2,)),
-            pltpu.SemaphoreType.DMA((2,)),
+            pltpu.SemaphoreType.DMA((2, 4)),
             pltpu.SemaphoreType.DMA((2,)),
             pltpu.SemaphoreType.DMA((2,)),
             pltpu.SemaphoreType.DMA((2,)),
@@ -598,6 +604,7 @@
             pltpu.SemaphoreType.DMA((4, 3)),
             pltpu.SemaphoreType.DMA((2,)),
             pltpu.SemaphoreType.DMA((2,)),
+            pltpu.SemaphoreType.REGULAR,
             pltpu.SemaphoreType.DMA((8,)),
         ],
         compiler_params=pltpu.CompilerParams(

time: 108 us -> 101 us (0.935); the launches traced: 106 us -> 101 us
  Pallas kernels: 99.1 us -> 94 us
    pallas_call x1, Pallas kernels: 99.1 us -> 94 us  [on_device(): pl.pallas_call(kernel, out_shape=(field, field), in_specs=[anyspec] * 3 +...]
where the time goes in v3:
time: 101 us
  Pallas kernels  94 us (93%)
  local copies, waits for them, and re-layouts  5.98 us (6%)
    pallas_call x1, Pallas kernels, on_device(): pl.pallas_call(kernel, out_shape=(field, field), in_specs=[anyspec] * 3 +...  94 us
    unnamed x5, local copies, waits for them, and re-layouts  5.98 us

profile of v3, /device:TPU:1, one launch (start us, length us, event | category | flops | bytes accessed | tf_op | source)
XLA Modules:
  0.0 100.6 jit_solution(5155285019606834200)
XLA Ops:
  0.6 1.3 %copy.11.st_ref = s32[8,4]{1,0:T(8,128)} copy(s32[8,4]{0,1:T(4,128)} %param.13) | data formatting | bytes 256 | tf_op args[4]
  2.0 94.0 %conjugate_gradient.1 = (f32[64,4,2048]{2,1,0:T(4,128)}, f32[64,4,2048]{2,1,0:T(4,128)}) custom-call(f32[64,4,2048]{2,1,0:T(4,128)} %b_hbm.1, f32[64,4,2048]{2,1,0:T(4,128)} %s_hbm.1, bf16[5,64,16,128]{3,2,1,0:T(8,128)(2,1)} %mem_hbm.1, f32[64,64]{1,0:T(8,128)} %root_ref.1, f32[48,256]{1,0:T(8,128)} %constant.6.clone.coef_ref, ...), custom_call_target="tpu_custom_call" | custom-call | tf_op jit(solution)/shard_map/conjugate_gradient/pallas_call | solution.py:562
  96.0 0.0 copy-start
  96.0 3.3 %copy.14 = f32[64,4,2048]{2,1,0:T(4,128)} copy(f32[64,4,2048]{2,1,0:T(4,128)} %get-tuple-element.4) | data formatting | bytes 4194304
  99.3 0.0 copy-done
  99.3 1.3 %copy.15 = f32[64,4,2048]{2,1,0:T(4,128)} copy(f32[64,4,2048]{2,1,0:T(4,128)S(1)} %copy-done) | data formatting | bytes 4194304
Async XLA Ops:
  96.0 3.3 %copy-start = (f32[64,4,2048]{2,1,0:T(4,128)S(1)}, f32[64,4,2048]{2,1,0:T(4,128)}, u32[]{:S(2)}) copy-start(f32[64,4,2048]{2,1,0:T(4,128)} %get-tuple-element.5) | copy-start | bytes 6291460

commit v4 on v3

--- a/solution.py
+++ b/solution.py
@@ -66,9 +66,9 @@
 
 
 def kernel(
-    b_hbm, s_hbm, mem_hbm, root_ref, coef_ref, xop, perm, st_ref, w_hbm, sol_hbm, res_hbm,
-    bv, sv, ab, mraw, wide_t, wide_g, halo_send, halo_recv, mem, amat, wv, fb, onehot, send_c, recv_c, own_c, u, ens, es, rs, zs, back, hs, outv,
-    part, sc1, sc2, sc3,
+    b_hbm, s_hbm, mem_hbm, root_hbm, coef_hbm, xop_hbm, perm_hbm, st_hbm, w_hbm, sol_hbm, res_hbm,
+    root_ref, coef_ref, xop, perm, st_ref, bv, sv, ab, mraw, wide_t, wide_g, halo_send, halo_recv, mem, amat, wv, fb, onehot, send_c, recv_c, own_c, u, ens, es, rs, zs, back, hs, outv,
+    part, sums,
     load_sem, a_send, a_recv, b_send, b_recv, c_send, c_recv, s_send, s_recv, h_send, h_recv, ready, out_sem,
 ):
     me = lax.axis_index("tile")
@@ -100,8 +100,12 @@
     for r in range(4):
         loads.append(pltpu.make_async_copy(s_hbm.at[:, r, :], sv.at[r], load_sem.at[5 + r]))
     loads.append(pltpu.make_async_copy(mem_hbm, mraw, load_sem.at[9]))
-    loads[9].start()
-    for load in loads[:9]:
+    loads.append(pltpu.make_async_copy(perm_hbm, perm, load_sem.at[10]))
+    loads.append(pltpu.make_async_copy(st_hbm, st_ref, load_sem.at[11]))
+    loads.append(pltpu.make_async_copy(root_hbm, root_ref, load_sem.at[12]))
+    loads.append(pltpu.make_async_copy(coef_hbm, coef_ref, load_sem.at[13]))
+    loads.append(pltpu.make_async_copy(xop_hbm, xop, load_sem.at[14]))
+    for load in loads[9:11] + loads[:9] + loads[11:]:
         load.start()
 
     def build():
@@ -111,8 +115,8 @@
         eye1 = (lanes_at == rows_at + LEV).astype(F32)
         for s in range(STENCIL):
             for q in range(4):
-                e0 = st_ref[q, s]
-                e1 = st_ref[4 + q, s]
+                e0 = st_ref[s, q]
+                e1 = st_ref[s, 4 + q]
 
                 def place(j, carry, s=s, q=q, e0=e0, e1=e1):
                     h0 = jnp.where(e0 == j, 1.0, 0.0).astype(F32)
@@ -187,7 +191,7 @@
             rows = []
             for q in range(4):
                 for i in range(2):
-                    rows.append(fb[st_ref[4 * i + q, s]])
+                    rows.append(fb[st_ref[s, 4 * i + q]])
             term = jnp.dot(jnp.concatenate(rows, axis=0), wv[s], preferred_element_type=F32)
             acc = term if acc is None else acc + term
         for q in range(4):
@@ -230,22 +234,26 @@
     def wait_c(it):
         wait_bytes(send_c.at[it, 0 : TILES - 1], a_send.at[it])
 
-    low = lax.rem(me, 8)
-    high = lax.div(me, 8)
+    def sum_peers(x):
+        return 16 if x % 2 else 8
+
+    def sum_place(x, stage):
+        if x % 2:
+            return mm * 4 + lax.rem(me, 4) if stage == 0 else lax.div(me, 4)
+        return lax.rem(me, 8) if stage == 0 else lax.div(me, 8)
 
     def sum_copy(x, stage, k):
-        if stage == 0:
-            slot, dst = low, sc1
-            to = at_tile(high * 8 + lax.rem(low + k, 8))
-        elif stage == 1:
-            slot, dst = high, sc2
-            to = at_tile(lax.rem(high + k, 8) * 8 + low)
+        peer = lax.rem(sum_place(x, stage) + k, sum_peers(x))
+        if x % 2:
+            if stage == 0:
+                to = {"tile": lax.div(me, 4) * 4 + lax.rem(peer, 4), "mem": lax.div(peer, 4)}
+            else:
+                to = at_tile(peer * 4 + lax.rem(me, 4))
         else:
-            slot, dst = mm, sc3
-            to = at_mem(lax.rem(mm + k, MEMS))
+            to = at_tile(lax.div(me, 8) * 8 + peer if stage == 0 else peer * 8 + lax.rem(me, 8))
         return pltpu.make_async_remote_copy(
             src_ref=part.at[x, stage],
-            dst_ref=dst.at[x, slot],
+            dst_ref=sums.at[x, stage, sum_place(x, stage)],
             send_sem=s_send.at[x, stage],
             recv_sem=s_recv.at[x, stage],
             device_id=to,
@@ -254,25 +262,18 @@
 
     def sum_start(x, stage, value):
         part[x, stage] = value
-        if stage == 0:
-            sc1[x, low] = value
-        elif stage == 1:
-            sc2[x, high] = value
-        else:
-            sc3[x, mm] = value
+        sums[x, stage, sum_place(x, stage)] = value
 
         def go(k, carry):
             sum_copy(x, stage, k).start()
             return carry
 
-        lax.fori_loop(1, MEMS if stage == 2 else 8, go, 0)
+        lax.fori_loop(1, sum_peers(x), go, 0)
 
     def sum_end(x, stage):
-        held = (sc1, sc2, sc3)[stage]
-        count = MEMS - 1 if stage == 2 else 7
-        wait_bytes(held.at[x, 0:count], s_recv.at[x, stage])
-        wait_bytes(held.at[x, 0:count], s_send.at[x, stage])
-        return jnp.sum(held[x], axis=0)
+        wait_bytes(sums.at[x, stage, 0 : sum_peers(x) - 1], s_recv.at[x, stage])
+        wait_bytes(sums.at[x, stage, 0 : sum_peers(x) - 1], s_send.at[x, stage])
+        return jnp.sum(sums[x, stage, 0 : sum_peers(x)], axis=0)
 
     def stack_rows(rows):
         rows = rows + [jnp.zeros((8 - len(rows), 128), F32)]
@@ -433,6 +434,7 @@
         return total
 
     loads[9].wait()
+    loads[10].wait()
     lax.fori_loop(0, LOCAL, turn, 0)
     pl.semaphore_wait(barrier, TILES - 1 + MEMS - 1)
 
@@ -448,6 +450,8 @@
         loads[r].wait()
         fill_blocks(r, bv[r].astype(BF16))
     loads[4].wait()
+    for load in loads[11:]:
+        load.wait()
     restrict(0)
     start_c(0)
     for r in range(4):
@@ -461,7 +465,6 @@
     sum_start(0, 0, stack_rows([square, diag]))
     build()
     wait_halo()
-    sum_start(0, 1, sum_end(0, 0))
     pl.semaphore_wait(ready, MEMS - 1)
     ensemble(0)
 
@@ -469,13 +472,13 @@
         return pack_row(ens[...] * recv_c[c_it, :, 0:16, :].astype(F32))
 
     sum_start(1, 0, stack_rows([col_dot(0)]))
+    sum_start(0, 1, sum_end(0, 0))
     wait_c(0)
-    first_sums = sum_end(0, 1)
     sum_start(1, 1, sum_end(1, 0))
     wait_rs(0)
-    sum_start(1, 2, sum_end(1, 1))
     start_back(0)
-    second_sums = sum_end(1, 2)
+    first_sums = sum_end(0, 1)
+    second_sums = sum_end(1, 1)
     rr = pick(first_sums, 0)
     dad = pick(first_sums, 1) + pick(second_sums, 0)
     alpha = rr / dad
@@ -503,17 +506,16 @@
                 cross = cross + pack_row(d * rnew * factor)
     sum_start(2, 0, stack_rows([square, diag, cross]))
     restrict(1)
-    sum_start(2, 1, sum_end(2, 0))
     start_c(1)
     ensemble(1)
     sum_start(3, 0, stack_rows([col_dot(1), col_dot(0)]))
+    sum_start(2, 1, sum_end(2, 0))
     wait_c(1)
-    third_sums = sum_end(2, 1)
     sum_start(3, 1, sum_end(3, 0))
     wait_rs(1)
-    sum_start(3, 2, sum_end(3, 1))
     start_back(1)
-    fourth_sums = sum_end(3, 2)
+    third_sums = sum_end(2, 1)
+    fourth_sums = sum_end(3, 1)
     new = pick(third_sums, 0)
     beta = new / rr
     both = pick(third_sums, 2) + pick(fourth_sums, 1)
@@ -546,6 +548,22 @@
         store.wait()
 
 
+def place(a_ref, b_ref, sol_ref, res_ref, held, in_sems, out_sems):
+    reads, writes = [], []
+    for part in range(4):
+        rows = pl.ds(16 * part, 16)
+        for n, (source, target) in enumerate(((a_ref, sol_ref), (b_ref, res_ref))):
+            reads.append(pltpu.make_async_copy(source.at[rows], held.at[n, rows], in_sems.at[n, part]))
+            writes.append(pltpu.make_async_copy(held.at[n, rows], target.at[rows], out_sems.at[n, part]))
+    for read in reads:
+        read.start()
+    for read, write in zip(reads, writes):
+        read.wait()
+        write.start()
+    for write in writes:
+        write.wait()
+
+
 def on_device(right_side, static_var, members, vertical_root, stencil, weights):
     coef = np.repeat(row_blocks().reshape(44, 4), LEV, axis=1)
     coef = jnp.asarray(np.concatenate([coef, np.zeros((4, 256))]), F32)
@@ -556,15 +574,19 @@
                 order[i * 64 + par * PAIRS + pair, 4 * pair + 2 * par + i] = 1.0
     perm = jnp.asarray(order, BF16)
     xop = jnp.asarray(column_operator(), BF16)
-    vmem = pl.BlockSpec(memory_space=pltpu.VMEM)
     anyspec = pl.BlockSpec(memory_space=pl.ANY)
     field = jax.ShapeDtypeStruct(right_side.shape, F32)
-    return pl.pallas_call(
+    fields = pl.pallas_call(
         kernel,
         out_shape=(field, field),
-        in_specs=[anyspec] * 3 + [vmem] * 4 + [pl.BlockSpec(memory_space=pltpu.SMEM), anyspec],
+        in_specs=[anyspec] * 9,
         out_specs=(anyspec, anyspec),
         scratch_shapes=[
+            pltpu.VMEM((LEV, LEV), F32),
+            pltpu.VMEM((48, 256), F32),
+            pltpu.VMEM((128, 256), BF16),
+            pltpu.VMEM((128, 128), BF16),
+            pltpu.SMEM((STENCIL, 8), jnp.int32),
             pltpu.VMEM((4, LEV, 2048), F32),
             pltpu.VMEM((4, LEV, 2048), F32),
             pltpu.VMEM((4, LEV, 2048), F32),
@@ -589,19 +611,17 @@
             pltpu.VMEM((2, TILES, 16, 128), BF16),
             pltpu.VMEM((STENCIL, 512, 256), BF16),
             pltpu.VMEM((2, 4, LEV, 2048), F32),
-            pltpu.VMEM((4, 3, 8, 128), F32),
-            pltpu.VMEM((4, 8, 8, 128), F32),
-            pltpu.VMEM((4, 8, 8, 128), F32),
-            pltpu.VMEM((4, MEMS, 8, 128), F32),
-            pltpu.SemaphoreType.DMA((12,)),
+            pltpu.VMEM((4, 2, 8, 128), F32),
+            pltpu.VMEM((4, 2, 16, 8, 128), F32),
+            pltpu.SemaphoreType.DMA((15,)),
             pltpu.SemaphoreType.DMA((2,)),
             pltpu.SemaphoreType.DMA((2, 4)),
             pltpu.SemaphoreType.DMA((2,)),
             pltpu.SemaphoreType.DMA((2,)),
             pltpu.SemaphoreType.DMA((2,)),
             pltpu.SemaphoreType.DMA((2,)),
-            pltpu.SemaphoreType.DMA((4, 3)),
-            pltpu.SemaphoreType.DMA((4, 3)),
+            pltpu.SemaphoreType.DMA((4, 2)),
+            pltpu.SemaphoreType.DMA((4, 2)),
             pltpu.SemaphoreType.DMA((2,)),
             pltpu.SemaphoreType.DMA((2,)),
             pltpu.SemaphoreType.REGULAR,
@@ -611,7 +631,20 @@
             collective_id=0, has_side_effects=True, vmem_limit_bytes=58 * 1024 * 1024
         ),
         name="conjugate_gradient",
-    )(right_side, static_var, members, vertical_root, coef, xop, perm, stencil, weights)
+    )(right_side, static_var, members, vertical_root, coef, xop, perm, stencil.T, weights)
+    return pl.pallas_call(
+        place,
+        out_shape=(field, field),
+        in_specs=[anyspec] * 2,
+        out_specs=(anyspec, anyspec),
+        scratch_shapes=[
+            pltpu.VMEM((2,) + right_side.shape, F32),
+            pltpu.SemaphoreType.DMA((2, 4)),
+            pltpu.SemaphoreType.DMA((2, 4)),
+        ],
+        compiler_params=pltpu.CompilerParams(vmem_limit_bytes=58 * 1024 * 1024),
+        name="outputs",
+    )(*fields)
 
 
 def solution(mesh):

time: 101 us -> 94.6 us (0.937)
  local copies, waits for them, and re-layouts: 5.98 us -> 0 us
    unnamed x5 -> x0, local copies, waits for them, and re-layouts: 5.98 us -> none
    pallas_call x1 -> x2, Pallas kernels: 94 us -> 93.5 us  [the longest x1 90 us: on_device(): pl.pallas_call(kernel, out_shape=(field, field), in_specs=[anyspec] * 9,...]
where the time goes in v4:
time: 94.6 us; the launch traced here: 94.2 us
  Pallas kernels  93.5 us (99%)
    pallas_call x1, Pallas kernels, on_device(): pl.pallas_call(kernel, out_shape=(field, field), in_specs=[anyspec] * 9,...  90 us
    pallas_call x1, Pallas kernels, on_device(): pl.pallas_call(place, out_shape=(field, field), in_specs=[anyspec] * 2, o...  3.58 us

profile of v4, /device:TPU:1, one launch (start us, length us, event | category | flops | bytes accessed | tf_op | source)
XLA Modules:
  0.0 94.2 jit_solution(15792468663581522561)
XLA Ops:
  0.6 90.0 %conjugate_gradient.1 = (f32[64,4,2048]{2,1,0:T(4,128)}, f32[64,4,2048]{2,1,0:T(4,128)}) custom-call(f32[64,4,2048]{2,1,0:T(4,128)} %b_hbm.1, f32[64,4,2048]{2,1,0:T(4,128)} %s_hbm.1, bf16[5,64,16,128]{3,2,1,0:T(8,128)(2,1)} %mem_hbm.1, f32[64,64]{1,0:T(8,128)} %root_hbm.1, f32[48,256]{1,0:T(8,128)} %constant.6.clone.coef_hbm, ...), custom_call_target="tpu_custom_call" | custom-call | tf_op jit(solution)/shard_map/conjugate_gradient/pallas_call | solution.py:579
  90.6 3.6 %outputs.1 = (f32[64,4,2048]{2,1,0:T(4,128)}, f32[64,4,2048]{2,1,0:T(4,128)}) custom-call(f32[64,4,2048]{2,1,0:T(4,128)} %get-tuple-element.4.a_ref, f32[64,4,2048]{2,1,0:T(4,128)} %get-tuple-element.5.b_ref), custom_call_target="tpu_custom_call" | custom-call | tf_op jit(solution)/shard_map/outputs/pallas_call | solution.py:635

commit v5 on v4

--- a/solution.py
+++ b/solution.py
@@ -83,16 +83,6 @@
     def at_mem(m):
         return {"tile": me, "mem": m}
 
-    barrier = pltpu.get_barrier_semaphore()
-
-    def greet(k, carry):
-        pl.semaphore_signal(barrier, inc=1, device_id=at_tile(lax.rem(me + k, TILES)), device_id_type=MESH)
-        return carry
-
-    lax.fori_loop(1, TILES, greet, 0)
-    for k in range(1, MEMS):
-        pl.semaphore_signal(barrier, inc=1, device_id=at_mem(lax.rem(mm + k, MEMS)), device_id_type=MESH)
-
     loads = []
     for r in range(4):
         loads.append(pltpu.make_async_copy(b_hbm.at[:, r, :], bv.at[r], load_sem.at[r]))
@@ -105,7 +95,18 @@
     loads.append(pltpu.make_async_copy(root_hbm, root_ref, load_sem.at[12]))
     loads.append(pltpu.make_async_copy(coef_hbm, coef_ref, load_sem.at[13]))
     loads.append(pltpu.make_async_copy(xop_hbm, xop, load_sem.at[14]))
-    for load in loads[9:11] + loads[:9] + loads[11:]:
+    for load in loads[9:11]:
+        load.start()
+    barrier = pltpu.get_barrier_semaphore()
+
+    def greet(k, carry):
+        pl.semaphore_signal(barrier, inc=1, device_id=at_tile(lax.rem(me + k, TILES)), device_id_type=MESH)
+        return carry
+
+    lax.fori_loop(1, TILES, greet, 0)
+    for k in range(1, MEMS):
+        pl.semaphore_signal(barrier, inc=1, device_id=at_mem(lax.rem(mm + k, MEMS)), device_id_type=MESH)
+    for load in loads[:9] + loads[11:]:
         load.start()
 
     def build():
@@ -322,11 +323,20 @@
         def _():
             pltpu.make_async_copy(es.at[it, t], rs.at[it, mm, slot], b_recv.at[it]).start()
 
+    def send_group(it, turn_at):
+        g = lax.rem(group_of_me + mm + 1 + turn_at, 4)
+
+        def go(k, carry):
+            out_go(it, g * QUARTER + lax.rem(me + k, QUARTER))
+            return carry
+
+        lax.fori_loop(0, QUARTER, go, 0)
+
     def ensemble(it):
         mix(it)
 
         def group(turn_at, carry):
-            g = lax.rem(me + mm + turn_at, 4)
+            g = lax.rem(group_of_me + mm + 1 + turn_at, 4)
             wide = []
             for m in range(LOCAL):
                 pieces = []
@@ -370,11 +380,10 @@
             both = jnp.stack([even, odd], axis=1).reshape(QUARTER, 16, 128).astype(BF16)
             es[it, pl.ds(g * QUARTER, QUARTER)] = both
 
-            def go(k, inner_carry):
-                out_go(it, g * QUARTER + lax.rem(me + k, QUARTER))
-                return inner_carry
-
-            lax.fori_loop(0, QUARTER, go, 0)
+            @pl.when(turn_at < 3)
+            def _():
+                send_group(it, turn_at)
+
             return carry
 
         lax.fori_loop(0, MEMS, group, 0)
@@ -472,6 +481,7 @@
         return pack_row(ens[...] * recv_c[c_it, :, 0:16, :].astype(F32))
 
     sum_start(1, 0, stack_rows([col_dot(0)]))
+    send_group(0, 3)
     sum_start(0, 1, sum_end(0, 0))
     wait_c(0)
     sum_start(1, 1, sum_end(1, 0))
@@ -482,6 +492,8 @@
     rr = pick(first_sums, 0)
     dad = pick(first_sums, 1) + pick(second_sums, 0)
     alpha = rr / dad
+    for r in range(4):
+        ab[r] = bv[r] * (1.0 + sv[r])
     wait_back(0)
     gather_back(0)
     square = jnp.zeros((1, 128), F32)
@@ -497,7 +509,7 @@
                 j = 4 * p + q
                 d = bv[r, :, cols]
                 factor = 1.0 + sv[r, :, cols]
-                image = d * factor + total[j * 64 : j * 64 + 64, :]
+                image = ab[r, :, cols] + total[j * 64 : j * 64 + 64, :]
                 ab[r, :, cols] = image
                 rnew = d - alpha * image
                 fb[j, :, piece * 256 : piece * 256 + 256] = rnew.astype(BF16)
@@ -509,6 +521,7 @@
     start_c(1)
     ensemble(1)
     sum_start(3, 0, stack_rows([col_dot(1), col_dot(0)]))
+    send_group(1, 3)
     sum_start(2, 1, sum_end(2, 0))
     wait_c(1)
     sum_start(3, 1, sum_end(3, 0))
@@ -521,9 +534,17 @@
     both = pick(third_sums, 2) + pick(fourth_sums, 1)
     dad2 = pick(third_sums, 1) + pick(fourth_sums, 0) + 2.0 * beta * both + beta * beta * dad
     alpha2 = new / dad2
+    stores = []
+    for r in range(4):
+        d = bv[r]
+        image = ab[r]
+        rnew = d - alpha * image
+        outv[0, r] = alpha * d + alpha2 * (rnew + beta * d)
+        outv[1, r] = rnew - alpha2 * (rnew * (1.0 + sv[r]) + beta * image)
+        stores.append(pltpu.make_async_copy(outv.at[0, r], sol_hbm.at[:, r, :], out_sem.at[r]))
+        stores[-1].start()
     wait_back(1)
     gather_back(1)
-    stores = []
     for piece in range(4):
         rr_, half = piece // 2, piece % 2
         total = prolong(piece)
@@ -532,17 +553,10 @@
                 r = 2 * p + rr_
                 cols = slice(q * 512 + half * 256, q * 512 + half * 256 + 256)
                 j = 4 * p + q
-                d = bv[r, :, cols]
-                image = ab[r, :, cols]
-                rnew = d - alpha * image
-                second = rnew * (1.0 + sv[r, :, cols]) + total[j * 64 : j * 64 + 64, :] + beta * image
-                outv[0, r, :, cols] = alpha * d + alpha2 * (rnew + beta * d)
-                outv[1, r, :, cols] = rnew - alpha2 * second
+                outv[1, r, :, cols] = outv[1, r, :, cols] - alpha2 * total[j * 64 : j * 64 + 64, :]
         if half == 1:
             for r in (rr_, 2 + rr_):
-                stores.append(pltpu.make_async_copy(outv.at[0, r], sol_hbm.at[:, r, :], out_sem.at[r]))
                 stores.append(pltpu.make_async_copy(outv.at[1, r], res_hbm.at[:, r, :], out_sem.at[4 + r]))
-                stores[-2].start()
                 stores[-1].start()
     for store in stores:
         store.wait()
@@ -550,8 +564,8 @@
 
 def place(a_ref, b_ref, sol_ref, res_ref, held, in_sems, out_sems):
     reads, writes = [], []
-    for part in range(4):
-        rows = pl.ds(16 * part, 16)
+    for part in range(2):
+        rows = pl.ds(32 * part, 32)
         for n, (source, target) in enumerate(((a_ref, sol_ref), (b_ref, res_ref))):
             reads.append(pltpu.make_async_copy(source.at[rows], held.at[n, rows], in_sems.at[n, part]))
             writes.append(pltpu.make_async_copy(held.at[n, rows], target.at[rows], out_sems.at[n, part]))
@@ -639,8 +653,8 @@
         out_specs=(anyspec, anyspec),
         scratch_shapes=[
             pltpu.VMEM((2,) + right_side.shape, F32),
-            pltpu.SemaphoreType.DMA((2, 4)),
-            pltpu.SemaphoreType.DMA((2, 4)),
+            pltpu.SemaphoreType.DMA((2, 8)),
+            pltpu.SemaphoreType.DMA((2, 8)),
         ],
         compiler_params=pltpu.CompilerParams(vmem_limit_bytes=58 * 1024 * 1024),
         name="outputs",

time: 94.6 us -> 93.1 us (0.984)
  Pallas kernels: 93.5 us -> 91.3 us
    pallas_call x1, Pallas kernels: 90 us -> 87.8 us  [on_device(): pl.pallas_call(kernel, out_shape=(field, field), in_specs=[anyspec] * 9,...]
where the time goes in v5:
time: 93.1 us; the launch traced here: 92.1 us
  Pallas kernels  91.3 us (98%)
    pallas_call x1, Pallas kernels, on_device(): pl.pallas_call(kernel, out_shape=(field, field), in_specs=[anyspec] * 9,...  87.8 us
    pallas_call x1, Pallas kernels, on_device(): pl.pallas_call(place, out_shape=(field, field), in_specs=[anyspec] * 2, o...  3.51 us

profile of v5, /device:TPU:1, one launch (start us, length us, event | category | flops | bytes accessed | tf_op | source)
XLA Modules:
  0.0 92.1 jit_solution(8881532854649399517)
XLA Ops:
  0.6 87.8 %conjugate_gradient.1 = (f32[64,4,2048]{2,1,0:T(4,128)}, f32[64,4,2048]{2,1,0:T(4,128)}) custom-call(f32[64,4,2048]{2,1,0:T(4,128)} %b_hbm.1, f32[64,4,2048]{2,1,0:T(4,128)} %s_hbm.1, bf16[5,64,16,128]{3,2,1,0:T(8,128)(2,1)} %mem_hbm.1, f32[64,64]{1,0:T(8,128)} %root_hbm.1, f32[48,256]{1,0:T(8,128)} %constant.6.clone.coef_hbm, ...), custom_call_target="tpu_custom_call" | custom-call | tf_op jit(solution)/shard_map/conjugate_gradient/pallas_call | solution.py:593
  88.4 3.5 %outputs.1 = (f32[64,4,2048]{2,1,0:T(4,128)}, f32[64,4,2048]{2,1,0:T(4,128)}) custom-call(f32[64,4,2048]{2,1,0:T(4,128)} %get-tuple-element.4.a_ref, f32[64,4,2048]{2,1,0:T(4,128)} %get-tuple-element.5.b_ref), custom_call_target="tpu_custom_call" | custom-call | tf_op jit(solution)/shard_map/outputs/pallas_call | solution.py:649

commit v6 on v5

--- a/solution.py
+++ b/solution.py
@@ -327,7 +327,7 @@
         g = lax.rem(group_of_me + mm + 1 + turn_at, 4)
 
         def go(k, carry):
-            out_go(it, g * QUARTER + lax.rem(me + k, QUARTER))
+            out_go(it, g * QUARTER + lax.rem(me + 5 * k, QUARTER))
             return carry
 
         lax.fori_loop(0, QUARTER, go, 0)

time: 93.1 us -> 93.6 us (level)
  no operation moved by 1% of the time
where the time goes in v6:
time: 93.6 us; the launch traced here: 92.6 us
  Pallas kernels  91.8 us (98%)
    pallas_call x1, Pallas kernels, on_device(): pl.pallas_call(kernel, out_shape=(field, field), in_specs=[anyspec] * 9,...  88.2 us
    pallas_call x1, Pallas kernels, on_device(): pl.pallas_call(place, out_shape=(field, field), in_specs=[anyspec] * 2, o...  3.51 us

profile of v6, /device:TPU:1, one launch (start us, length us, event | category | flops | bytes accessed | tf_op | source)
XLA Modules:
  0.0 92.6 jit_solution(5001594966835485822)
XLA Ops:
  0.6 88.2 %conjugate_gradient.1 = (f32[64,4,2048]{2,1,0:T(4,128)}, f32[64,4,2048]{2,1,0:T(4,128)}) custom-call(f32[64,4,2048]{2,1,0:T(4,128)} %b_hbm.1, f32[64,4,2048]{2,1,0:T(4,128)} %s_hbm.1, bf16[5,64,16,128]{3,2,1,0:T(8,128)(2,1)} %mem_hbm.1, f32[64,64]{1,0:T(8,128)} %root_hbm.1, f32[48,256]{1,0:T(8,128)} %constant.6.clone.coef_hbm, ...), custom_call_target="tpu_custom_call" | custom-call | tf_op jit(solution)/shard_map/conjugate_gradient/pallas_call | solution.py:593
  88.9 3.5 %outputs.1 = (f32[64,4,2048]{2,1,0:T(4,128)}, f32[64,4,2048]{2,1,0:T(4,128)}) custom-call(f32[64,4,2048]{2,1,0:T(4,128)} %get-tuple-element.4.a_ref, f32[64,4,2048]{2,1,0:T(4,128)} %get-tuple-element.5.b_ref), custom_call_target="tpu_custom_call" | custom-call | tf_op jit(solution)/shard_map/outputs/pallas_call | solution.py:649
